TPU v7x, 256 devices: a whole 4x4x8 slice. The times are simulated.
256 devices in a mesh: section: 8 (over y, z_hi), expert: 32 (over x, z_lo, core).
Axes of the slice: x: 4, y: 4, z: 8 (z_hi: 2, z_lo: 4; z = z_hi * 4 + z_lo), core: 2. Of those that a mesh axis runs over, the one named last changes fastest.
Arguments:
- act_fwd: bfloat16 [8, 4096, 4096], P('section', 'expert'), may hold values from -6 to 6
- act_rev: bfloat16 [8, 4096, 4096], P('section', 'expert'), may hold values from -6 to 6
- ids_fwd: int32 [8, 4096, 2], P('section', 'expert'), may hold values from 0 to 15, all different within a row; in each aligned block of 128 rows (0 to 127, 128 to 255, ..., all dimensions but the last counted through in order) at most 24 rows name the same one
- ids_rev: int32 [8, 4096, 2], P('section', 'expert'), may hold values from 0 to 15, all different within a row; in each aligned block of 128 rows (0 to 127, 128 to 255, ..., all dimensions but the last counted through in order) at most 24 rows name the same one
- probs_fwd: float32 [8, 4096, 2], P('section', 'expert'), may hold values from 0.05 to 1
- probs_rev: float32 [8, 4096, 2], P('section', 'expert'), may hold values from 0.05 to 1
- w_gate: bfloat16 [8, 4096, 12288], P('section', None, 'expert'), may hold values from -0.09375 to 0.09375
- w_up: bfloat16 [8, 4096, 12288], P('section', None, 'expert'), may hold values from -0.09375 to 0.09375
- w_down: bfloat16 [8, 12288, 4096], P('section', 'expert'), may hold values from -0.21875 to 0.21875
Outputs:
- out_fwd: bfloat16 [8, 4096, 4096], P('section', 'expert')
- out_rev: bfloat16 [8, 4096, 4096], P('section', 'expert')
Inputs may be any that keep to these rules, and one draw needn't show every extreme that they name: `ids_fwd`: each row names 2 different experts. Within the 128 rows of one device (aligned blocks) no expert is named by more than 24 rows, and some block reaches 24. `ids_rev`: as for ids_fwd.
All inputs are finite; a program needn't handle non-finite values.
Results may differ from a plain program's by a relative error of at most 0.0048.
Values may be sent and summed in bfloat16 or wider, within the bound.
No kernel may reach another device: no remote copies, remote signals or barrier semaphores. Data moves between devices by JAX's collectives and lax.ppermute only.
A program may use at most 128 MiB of HBM per device.

v0:
```python
import jax
import jax.numpy as jnp
from jax import lax
from jax.sharding import PartitionSpec as P


def from_behind(block, axis, distance):
    devices = range(lax.axis_size(axis))
    route = [((i - distance) % len(devices), i) for i in devices]
    return lax.ppermute(block, axis, route)


def expert_rows(received_rows, w_gate, w_up, w_down):
    model_width = received_rows.shape[-1]
    flat_rows = received_rows.reshape(-1, model_width)
    gate_pre = jnp.dot(flat_rows, w_gate[0], preferred_element_type=jnp.float32)
    up_pre = jnp.dot(flat_rows, w_up[0], preferred_element_type=jnp.float32)
    hidden = (jax.nn.silu(gate_pre) * up_pre).astype(jnp.bfloat16)
    partial_value = jnp.dot(hidden, w_down[0], preferred_element_type=jnp.float32).astype(
        jnp.bfloat16
    )
    return partial_value.reshape(received_rows.shape)


def moe_layer(tokens_in, route_ids, probs, w_gate, w_up, w_down):
    tok_count, route_count = route_ids.shape
    model_width = tokens_in.shape[1]
    device_count = lax.axis_size("expert")
    expert_count = device_count // 2
    slot_count = 2 * (3 * tok_count * route_count // (4 * expert_count))
    flat_ids = route_ids.reshape(-1)
    one_hot = (flat_ids[:, None] == jnp.arange(expert_count, dtype=jnp.int32)[None, :]).astype(
        jnp.int32
    )
    rank_in = jnp.sum((jnp.cumsum(one_hot, axis=0) - 1) * one_hot, axis=1)
    slot_of = flat_ids * slot_count + rank_in
    slot_range = jnp.arange(expert_count * slot_count, dtype=jnp.int32)
    pick_rows = (slot_range[:, None] == slot_of[None, :]).astype(jnp.bfloat16)
    pick_tokens = jnp.sum(
        pick_rows.reshape(expert_count * slot_count, tok_count, route_count), axis=2
    )
    outgoing = jnp.dot(pick_tokens, tokens_in, preferred_element_type=jnp.float32).astype(
        jnp.bfloat16
    )
    outgoing_all = jnp.repeat(outgoing.reshape(expert_count, slot_count, model_width), 2, axis=0)
    partial_value = expert_rows(
        lax.all_to_all(outgoing_all, "expert", split_axis=0, concat_axis=0, tiled=True),
        w_gate,
        w_up,
        w_down,
    )
    returned = lax.all_to_all(partial_value, "expert", split_axis=0, concat_axis=0, tiled=True)
    paired_sum = jnp.sum(
        returned.reshape(expert_count, 2, slot_count, model_width).astype(jnp.float32), axis=1
    )
    expert_out = paired_sum.astype(jnp.bfloat16).reshape(expert_count * slot_count, model_width)
    route_pick = (slot_of[:, None] == slot_range[None, :]).astype(jnp.bfloat16)
    per_route = jnp.dot(route_pick, expert_out, preferred_element_type=jnp.float32)
    weights = probs / jnp.sum(probs, axis=1, keepdims=True)
    mixed = tokens_in.astype(jnp.float32) + jnp.sum(
        per_route.reshape(tok_count, route_count, model_width) * weights[:, :, None], axis=1
    )
    return mixed.astype(jnp.bfloat16)


def body(act_fwd, act_rev, ids_fwd, ids_rev, probs_fwd, probs_rev, w_gate, w_up, w_down):
    arrived_fwd = from_behind(act_fwd, "section", 1)
    arrived_rev = from_behind(act_rev, "section", -1)
    out_fwd = moe_layer(arrived_fwd[0], ids_fwd[0], probs_fwd[0], w_gate, w_up, w_down)
    out_rev = moe_layer(arrived_rev[0], ids_rev[0], probs_rev[0], w_gate, w_up, w_down)
    return (out_fwd[None], out_rev[None])


def solution(mesh):
    return jax.shard_map(
        body,
        mesh=mesh,
        in_specs=(
            P("section", "expert", None),
            P("section", "expert", None),
            P("section", "expert", None),
            P("section", "expert", None),
            P("section", "expert", None),
            P("section", "expert", None),
            P("section", None, "expert"),
            P("section", None, "expert"),
            P("section", "expert", None),
        ),
        out_specs=(P("section", "expert", None), P("section", "expert", None)),
        check_vma=False,
    )
```

profile of v0, /device:TPU:1, one launch (start us, length us, event | category | flops | bytes accessed | tf_op | source)
XLA Modules:
  0.0 704.3 jit_solution(7619547573678784648)
XLA Ops:
  0.6 0.0 copy-start
  0.6 10.3 %collective-permute-start.1 = (bf16[1,128,4096]{2,1,0:T(8,128)(2,1)}, bf16[1,128,4096]{2,1,0:T(8,128)(2,1)}, u32[]{:S(2)}, u32[]{:S(2)}) collective-permute-start(bf16[1,128,4096]{2,1,0:T(8,128)(2,1)} %param.10), channel_id=1, source_target_pairs={{32,0},{64,32},{96,64},{128,96},{160,128},{192,160},{224,192},{0,2... | collective-permute-start | bytes 3145736 | tf_op jit(solution)/shard_map/ppermute | solution.py:10
  10.9 0.8 copy.29
  11.7 0.1 eq.155
  11.8 0.1 eq.151
  12.0 0.6 reduce-window.16
  12.6 0.2 slice_reduce_fusion
  12.8 0.1 fusion.39
  12.9 0.1 reduce_sum.118
  13.1 0.1 copy.33
  13.1 0.1 fusion.34
  13.2 41.8 %collective-permute-done.1 = bf16[1,128,4096]{2,1,0:T(8,128)(2,1)} collective-permute-done((bf16[1,128,4096]{2,1,0:T(8,128)(2,1)}, bf16[1,128,4096]{2,1,0:T(8,128)(2,1)}, u32[]{:S(2)}, u32[]{:S(2)}) %collective-permute-start.1) | collective-permute-done | bytes 1048608 | tf_op jit(solution)/shard_map/ppermute | solution.py:10
  55.0 2.2 convolution_convert_fusion.2
  57.2 3.4 broadcast_in_dim.5
  60.6 7.2 %all-to-all-start.2 = ((bf16[32,24,4096]{2,1,0:T(8,128)(2,1)}), bf16[32,24,4096]{2,1,0:T(8,128)(2,1)}, u32[]{:S(2)}, u32[]{:S(2)}) async-start(bf16[32,24,4096]{2,1,0:T(8,128)(2,1)} %bitcast.109), calls=%async_computation.2 | async-start | bytes 12582912 | tf_op jit(solution)/shard_map/all_to_all | solution.py:47
  67.8 5.0 collective-permute-start
  72.8 0.1 copy.23
  72.9 0.1 eq.140
  73.0 0.1 eq.136
  73.2 0.6 reduce-window.14
  73.8 0.2 slice_reduce_fusion.1
  74.0 0.1 fusion.41
  74.1 0.1 reduce_sum.111
  74.3 0.1 copy.27
  74.3 0.1 fusion.35
  74.4 150.5 %collective-permute-done = bf16[1,128,4096]{2,1,0:T(8,128)(2,1)} collective-permute-done((bf16[1,128,4096]{2,1,0:T(8,128)(2,1)}, bf16[1,128,4096]{2,1,0:T(8,128)(2,1)}, u32[]{:S(2)}, u32[]{:S(2)}) %collective-permute-start) | collective-permute-done | bytes 1048608 | tf_op jit(solution)/shard_map/ppermute | solution.py:10
  224.9 3.9 convolution_convert_fusion.3
  228.8 23.4 %all-to-all-done.2 = bf16[32,24,4096]{2,1,0:T(8,128)(2,1)} async-done(((bf16[32,24,4096]{2,1,0:T(8,128)(2,1)}), bf16[32,24,4096]{2,1,0:T(8,128)(2,1)}, u32[]{:S(2)}, u32[]{:S(2)}) %all-to-all-start.2) | async-done | bytes 6291488 | tf_op jit(solution)/shard_map/all_to_all | solution.py:47
  252.2 5.3 broadcast_in_dim.4
  257.5 5.7 all-to-all-start
  263.2 6.6 fusion.6
  269.8 6.3 fusion.20
  276.1 5.3 convolution_convert_fusion
  281.4 121.3 %all-to-all-done = bf16[32,24,4096]{2,1,0:T(8,128)(2,1)} async-done(((bf16[32,24,4096]{2,1,0:T(8,128)(2,1)}), bf16[32,24,4096]{2,1,0:T(8,128)(2,1)}, u32[]{:S(2)}, u32[]{:S(2)}) %all-to-all-start) | async-done | bytes 6291488 | tf_op jit(solution)/shard_map/all_to_all | solution.py:47
  402.7 5.7 all-to-all-start.3
  408.5 6.6 fusion.8
  415.1 6.3 fusion.23
  421.3 5.4 convolution_convert_fusion.1
  426.8 121.2 %all-to-all-done.3 = bf16[32,24,4096]{2,1,0:T(8,128)(2,1)} async-done(((bf16[32,24,4096]{2,1,0:T(8,128)(2,1)}), bf16[32,24,4096]{2,1,0:T(8,128)(2,1)}, u32[]{:S(2)}, u32[]{:S(2)}) %all-to-all-start.3) | async-done | bytes 6291488 | tf_op jit(solution)/shard_map/all_to_all | solution.py:52
  548.0 5.9 all-to-all-start.1
  553.9 4.4 bitcast_reduce_fusion
  558.4 2.8 fusion.13
  561.2 132.1 %all-to-all-done.1 = bf16[32,24,4096]{2,1,0:T(8,128)(2,1)} async-done(((bf16[32,24,4096]{2,1,0:T(8,128)(2,1)}), bf16[32,24,4096]{2,1,0:T(8,128)(2,1)}, u32[]{:S(2)}, u32[]{:S(2)}) %all-to-all-start.1) | async-done | bytes 6291488 | tf_op jit(solution)/shard_map/all_to_all | solution.py:52
  693.4 4.4 bitcast_reduce_fusion.1
  697.8 1.5 fusion.12
  699.3 0.1 copy-done.1
  699.4 2.4 fusion.10
  701.8 2.4 fusion.11
  (24 shorter events, 0.2 us)
Async XLA Ops:
  0.6 275.5 %copy-start = (bf16[1,384,4096]{2,1,0:T(8,128)(2,1)S(1)}, bf16[1,384,4096]{2,1,0:T(8,128)(2,1)}, u32[]{:S(2)}) copy-start(bf16[1,384,4096]{2,1,0:T(8,128)(2,1)} %param.17) | copy-start | bytes 9437188
  0.6 54.3 %collective-permute-start.1 = (bf16[1,128,4096]{2,1,0:T(8,128)(2,1)}, bf16[1,128,4096]{2,1,0:T(8,128)(2,1)}, u32[]{:S(2)}, u32[]{:S(2)}) collective-permute-start(bf16[1,128,4096]{2,1,0:T(8,128)(2,1)} %param.10), channel_id=1, source_target_pairs={{32,0},{64,32},{96,64},{128,96},{160,128},{192,160},{224,192},{0,2... | collective-permute-start | bytes 3145736 | tf_op jit(solution)/shard_map/ppermute | solution.py:10
  60.6 12.2 %copy-start.4 = (s32[1,128,2]{1,2,0:T(2,128)S(1)}, s32[1,128,2]{1,2,0:T(2,128)}, u32[]{:S(2)}) copy-start(s32[1,128,2]{1,2,0:T(2,128)} %param.11) | copy-start | bytes 3076
  60.6 191.6 %all-to-all-start.2 = ((bf16[32,24,4096]{2,1,0:T(8,128)(2,1)}), bf16[32,24,4096]{2,1,0:T(8,128)(2,1)}, u32[]{:S(2)}, u32[]{:S(2)}) async-start(bf16[32,24,4096]{2,1,0:T(8,128)(2,1)} %bitcast.109), calls=%async_computation.2 | async-start | bytes 12582912 | tf_op jit(solution)/shard_map/all_to_all | solution.py:47
  67.8 157.1 %collective-permute-start = (bf16[1,128,4096]{2,1,0:T(8,128)(2,1)}, bf16[1,128,4096]{2,1,0:T(8,128)(2,1)}, u32[]{:S(2)}, u32[]{:S(2)}) collective-permute-start(bf16[1,128,4096]{2,1,0:T(8,128)(2,1)} %param.9), channel_id=1, source_target_pairs={{224,0},{0,32},{32,64},{64,96},{96,128},{128,160},{160,192},{192,2... | collective-permute-start | bytes 3145736 | tf_op jit(solution)/shard_map/ppermute | solution.py:10
  257.5 145.2 %all-to-all-start = ((bf16[32,24,4096]{2,1,0:T(8,128)(2,1)}), bf16[32,24,4096]{2,1,0:T(8,128)(2,1)}, u32[]{:S(2)}, u32[]{:S(2)}) async-start(bf16[32,24,4096]{2,1,0:T(8,128)(2,1)} %bitcast.110), calls=%async_computation | async-start | bytes 12582912 | tf_op jit(solution)/shard_map/all_to_all | solution.py:47
  263.2 6.6 copy-start.5
  402.7 145.2 %all-to-all-start.3 = ((bf16[32,24,4096]{2,1,0:T(8,128)(2,1)}), bf16[32,24,4096]{2,1,0:T(8,128)(2,1)}, u32[]{:S(2)}, u32[]{:S(2)}) async-start(bf16[32,24,4096]{2,1,0:T(8,128)(2,1)} %bitcast.114), calls=%async_computation.3 | async-start | bytes 12582912 | tf_op jit(solution)/shard_map/all_to_all | solution.py:52
  408.4 6.6 copy-start.6
  548.0 5.9 copy-start.2
  548.0 5.9 copy-start.3
  548.0 145.4 %all-to-all-start.1 = ((bf16[32,24,4096]{2,1,0:T(8,128)(2,1)}), bf16[32,24,4096]{2,1,0:T(8,128)(2,1)}, u32[]{:S(2)}, u32[]{:S(2)}) async-start(bf16[32,24,4096]{2,1,0:T(8,128)(2,1)} %bitcast.113), calls=%async_computation.1 | async-start | bytes 12582912 | tf_op jit(solution)/shard_map/all_to_all | solution.py:52
  697.8 1.6 copy-start.1
where the time goes:
time: 705 us; the launch traced here: 704 us
  waiting for transfers between devices  590 us (84%)
  matrix products  46.9 us (7%)
  starting transfers between devices  39.7 us (6%)
  other arithmetic  15.4 us (2%)
  local copies, waits for them, and re-layouts  11.1 us (2%)
    all_to_all x2, waiting for transfers between devices, moe_layer(): lax.all_to_all(partial_value, 'expert', split_axis=0, concat_axis=0, tile...  253 us
    ppermute x2, waiting for transfers between devices, from_behind(): return lax.ppermute(block, axis, route)  192 us
    all_to_all x2, waiting for transfers between devices, moe_layer(): lax.all_to_all(outgoing_all, 'expert', split_axis=0, concat_axis=0, tiled...  145 us
    ppermute x2, starting transfers between devices, from_behind(): return lax.ppermute(block, axis, route)  15.2 us
  transfers between devices with their start and end apart: 6, of which 6 were waited for; matrix products, arithmetic and copies ran while one was open for 7% of the time, Pallas kernels for 0%

commit v1 on v0

v1 whole, which is shorter than its diff:
```python
import jax
import jax.numpy as jnp
from jax import lax
from jax.sharding import Mesh
from jax.sharding import PartitionSpec as P

EXPERTS = 16
CAP = 24
X, Z, Y = 4, 4, 4
BF = jnp.bfloat16
F32 = jnp.float32


def slots_of(ids):
    flat = ids.reshape(-1)
    n = flat.shape[0]
    one_hot = (flat[:, None] == jnp.arange(EXPERTS, dtype=jnp.int32)[None, :]).astype(BF)
    place = jnp.arange(n, dtype=jnp.int32)
    below = (place[:, None] > place[None, :]).astype(BF)
    counts = jnp.dot(below, one_hot, preferred_element_type=F32)
    rank = jnp.sum(counts * one_hot.astype(F32), axis=1).astype(jnp.int32)
    return (flat * CAP + rank).reshape(ids.shape)


def outgoing(tokens, slots, z_lo):
    t = slots.shape[1]
    row = jnp.arange(X * Z * CAP, dtype=jnp.int32)
    to_x, source, rank = row // (Z * CAP), row // CAP % Z, row % CAP
    target = (to_x * Z + z_lo) * CAP + rank
    held = jnp.arange(Z * t, dtype=jnp.int32) // t
    flat = slots.reshape(Z * t, 2)
    hit = (flat[None, :, 0] == target[:, None]) | (flat[None, :, 1] == target[:, None])
    pick = (hit & (held[None, :] == source[:, None])).astype(BF)
    return jnp.dot(pick, tokens, preferred_element_type=F32).astype(BF)


def expert(rows, w_gate, w_up, w_down):
    gate = jnp.dot(rows, w_gate, preferred_element_type=F32)
    up = jnp.dot(rows, w_up, preferred_element_type=F32)
    hidden = (jax.nn.silu(gate) * up).astype(BF)
    return jnp.dot(hidden, w_down, preferred_element_type=F32).astype(BF)


def combine(home, back, slots, probs):
    gates = probs / jnp.sum(probs, axis=1, keepdims=True)
    place = jnp.arange(EXPERTS * CAP, dtype=jnp.int32)
    mix = jnp.sum(
        jnp.where(slots[:, :, None] == place[None, None, :], gates[:, :, None], 0.0), axis=1
    )
    high = lax.reduce_precision(mix, 8, 7)
    both = jnp.concatenate([high, mix - high], axis=0).astype(BF)
    summed = jnp.dot(both, back, preferred_element_type=F32)
    t = home.shape[0]
    return (home.astype(F32) + (summed[:t] + summed[t:])).astype(BF)


def after(value, *others):
    return lax.optimization_barrier((value, *others))[0]


def body(act_fwd, act_rev, ids_fwd, ids_rev, probs_fwd, probs_rev, w_gate, w_up, w_down):
    z_hi, z_lo = lax.axis_index("z_hi"), lax.axis_index("z_lo")
    upper = z_hi == 1
    act_fwd, act_rev = act_fwd[0], act_rev[0]
    t, d = act_fwd.shape

    def choose(a, b):
        return jnp.where(upper, a, b)

    first = choose(act_rev, act_fwd)
    hop = [((y - 1) % Y * 2 + 1, y * 2 + 1) for y in range(Y)]
    hop += [((y + 1) % Y * 2, y * 2) for y in range(Y)]
    second = lax.ppermute(choose(act_fwd, act_rev), ("y", "z_hi"), hop)

    def ring(block):
        full = lax.all_gather(block, ("z_hi", "z_lo"), axis=0, tiled=True)
        return full

    def arrived(full):
        return lax.dynamic_slice_in_dim(full, (1 - z_hi) * Z * t, Z * t, 0)

    def at_home(full):
        return lax.dynamic_slice_in_dim(full, ((1 - z_hi) * Z + z_lo) * t, t, 0)

    full_1 = ring(first)

    ids = [choose(ids_fwd[0], ids_rev[0]), choose(ids_rev[0], ids_fwd[0])]
    probs = [choose(probs_fwd[0], probs_rev[0]), choose(probs_rev[0], probs_fwd[0])]
    slots = [slots_of(i) for i in ids]
    slots_all = lax.all_gather(jnp.stack(slots), "z_lo", axis=0)

    swap = [(0, 1), (1, 0)]
    gate_w = jnp.concatenate([w_gate[0], lax.ppermute(w_gate[0], "core", swap)], axis=1)
    up_w = jnp.concatenate([w_up[0], lax.ppermute(w_up[0], "core", swap)], axis=1)
    down_w = jnp.concatenate([w_down[0], lax.ppermute(w_down[0], "core", swap)], axis=0)

    full_2 = ring(after(second, full_1))

    outs = []
    for p, full in enumerate((full_1, full_2)):
        sent = outgoing(arrived(full), slots_all[:, p], z_lo)
        rows = lax.all_to_all(sent, "x", split_axis=0, concat_axis=0, tiled=True)
        done = expert(rows, gate_w, up_w, down_w)
        back = lax.all_to_all(done, ("x", "z_lo"), split_axis=0, concat_axis=0, tiled=True)
        outs.append(combine(at_home(full), back, slots[p], probs[p]))

    return (choose(outs[0], outs[1])[None], choose(outs[1], outs[0])[None])


def solution(mesh):
    split = Mesh(mesh.devices.reshape(Y, 2, X, Z, 2), ("y", "z_hi", "x", "z_lo", "core"))
    section, spread = ("y", "z_hi"), ("x", "z_lo", "core")
    tokens = P(section, spread, None)
    return jax.shard_map(
        body,
        mesh=split,
        in_specs=(tokens,) * 6 + (P(section, None, spread),) * 2 + (tokens,),
        out_specs=(tokens, tokens),
        check_vma=False,
    )
```

time: 705 us -> 420 us (0.60)
  waiting for transfers between devices: 590 us -> 297 us
  starting transfers between devices: 39.7 us -> 24.4 us
  between operations: 0.9 us -> 14.3 us
  matrix products: 46.9 us -> 59.7 us
  blocking collectives: 0 us -> 11.1 us
    all_to_all x4, waiting for transfers between devices: 398 us -> 133 us  [the longest x2 116 us: body(): lax.all_to_all(done, ('x', 'z_lo'), split_axis=0, concat_axis=0, tiled=True)]
    ppermute x2 -> x4, waiting for transfers between devices: 192 us -> 21.8 us  [the longest x1 21.8 us: body(): second = lax.ppermute(choose(act_fwd, act_rev), ('y', 'z_hi'), hop)]
    all_gather x0 -> x2, waiting for transfers between devices: none -> 142 us  [ring(): full = lax.all_gather(block, ('z_hi', 'z_lo'), axis=0, tiled=True)]
    dot_general x10, matrix products: 46.9 us -> 59.7 us  [the longest x2 27.5 us: expert(): return jnp.dot(hidden, w_down, preferred_element_type=F32).astype(BF)]
    all_gather x0 -> x1, blocking collectives: none -> 11.1 us  [body(): slots_all = lax.all_gather(jnp.stack(slots), 'z_lo', axis=0)]
    ppermute x2 -> x4, starting transfers between devices: 15.2 us -> 6.23 us  [the longest x1 3.64 us: body(): second = lax.ppermute(choose(act_fwd, act_rev), ('y', 'z_hi'), hop)]
    reduce_sum x8 -> x3, other arithmetic: 9.26 us -> 0.4 us  [the longest x2 0.3 us: combine(): jnp.sum(jnp.where(slots[:, :, None] == place[None, None, :], gates[:, :,...]
    broadcast_in_dim x2 -> x0, local copies, waits for them, and re-layouts: 8.73 us -> none  [moe_layer(): jnp.repeat(outgoing.reshape(expert_count, slot_count, model_width), 2, ax...]
  transfers between devices with their start and end apart: 6 -> 10, of which waited for: 6 -> 6; matrix products, arithmetic and copies ran while one was open for 7% -> 15% of each run, Pallas kernels for 0% -> 0%
where the time goes in v1:
time: 420 us
  waiting for transfers between devices  297 us (71%)
  matrix products  59.7 us (14%)
  starting transfers between devices  24.4 us (6%)
  between operations  14.3 us (3%)
  blocking collectives  11.1 us (3%)
  other arithmetic  8.69 us (2%)
  local copies, waits for them, and re-layouts  4.35 us (1%)
    all_gather x2, waiting for transfers between devices, ring(): full = lax.all_gather(block, ('z_hi', 'z_lo'), axis=0, tiled=True)  142 us
    all_to_all x2, waiting for transfers between devices, body(): lax.all_to_all(done, ('x', 'z_lo'), split_axis=0, concat_axis=0, tiled=True)  116 us
    dot_general x2, matrix products, expert(): return jnp.dot(hidden, w_down, preferred_element_type=F32).astype(BF)  27.5 us
    ppermute x1, waiting for transfers between devices, body(): second = lax.ppermute(choose(act_fwd, act_rev), ('y', 'z_hi'), hop)  21.8 us
    all_to_all x2, waiting for transfers between devices, body(): rows = lax.all_to_all(sent, 'x', split_axis=0, concat_axis=0, tiled=True)  17 us
    dot_general x2, matrix products, expert(): up = jnp.dot(rows, w_up, preferred_element_type=F32)  13.8 us
    dot_general x2, matrix products, outgoing(): return jnp.dot(pick, tokens, preferred_element_type=F32).astype(BF)  11.4 us
    all_gather x1, blocking collectives, body(): slots_all = lax.all_gather(jnp.stack(slots), 'z_lo', axis=0)  11.1 us
  transfers between devices with their start and end apart: 10, of which 6 were waited for; matrix products, arithmetic and copies ran while one was open for 15% of the time, Pallas kernels for 0%

profile of v1, /device:TPU:1, one launch (start us, length us, event | category | flops | bytes accessed | tf_op | source)
XLA Modules:
  0.0 419.6 jit_solution(7810823616252128842)
XLA Ops:
  7.2 2.7 broadcast_select_fusion
  10.0 3.6 collective-permute-start.3
  13.6 21.8 %collective-permute-done.3 = bf16[128,4096]{1,0:T(8,128)(2,1)S(1)} collective-permute-done((bf16[128,4096]{1,0:T(8,128)(2,1)S(1)}, bf16[128,4096]{1,0:T(8,128)(2,1)S(1)}, u32[]{:S(2)}, u32[]{:S(2)}) %collective-permute-start.3) | collective-permute-done | bytes 1048608 | tf_op jit(solution)/shard_map/ppermute | solution.py:73
  35.4 1.0 copy-done.1
  36.4 1.6 collective-permute-start.1
  38.1 0.1 copy.37
  38.2 0.1 copy.38
  38.3 0.1 select_n.171
  38.5 0.2 fusion.11
  38.7 0.1 select_n.176
  38.8 0.2 fusion.12
  39.0 0.1 convert_element_type.97
  39.2 0.1 convert_element_type.93
  39.3 0.1 copy.46
  39.4 0.1 copy.45
  39.5 11.1 %all-gather.1 = s32[8,128,2]{1,2,0:T(2,128)S(1)} all-gather(s32[2,128,2]{1,2,0:T(2,128)S(1)} %pad_add_fusion), channel_id=3, replica_groups=mesh['y'=4,'z_hi'=2,'x'=4,'z_lo'=4,'core'=2] {'z_lo'}, dimensions={0}, use_global_device_ids=true | all-gather | bytes 10240 | tf_op jit(solution)/shard_map/all_gather | solution.py:90
  50.6 57.7 %all-gather.7.cloned.1.call-done = bf16[1,1024,4096]{2,1,0:T(8,128)(2,1)} async-done(((bf16[1,128,4096]{2,1,0:T(8,128)(2,1)}), bf16[1,1024,4096]{2,1,0:T(8,128)(2,1)}) %all-gather.7.cloned.1.call-update) | async-done | bytes 8388624 | tf_op jit(solution)/shard_map/all_gather | solution.py:76
  108.3 5.7 %convolution_convert_fusion.1 = bf16[384,4096]{1,0:T(8,128)(2,1)} fusion(bf16[1,1024,4096]{2,1,0:T(8,128)(2,1)} %all-gather.7.cloned.1.call-done, s32[]{:T(128)S(6)} %select_n.182, s32[512]{0:T(512)S(1)} %add_select_fusion.2, s32[512]{0:T(512)S(1)} %bitcast.58, s32[512]{0:T(512)S(1)} %bitcast.57, s32[384]{0:T(512)S(1)} %get-tuple-element.29, ...), kind=kOutput, calls=%fused_computation.4 | convolution fusion | flops 1613168640 | bytes 7349252 | tf_op jit(solution)/shard_map/dot_general | solution.py:34
  114.0 4.0 all-to-all-start
  118.0 1.0 collective-permute-start
  119.0 84.6 %all-gather.5.cloned.1.call-done = bf16[1024,4096]{1,0:T(8,128)(2,1)} async-done(((bf16[128,4096]{1,0:T(8,128)(2,1)}), bf16[1024,4096]{1,0:T(8,128)(2,1)}) %all-gather.5.cloned.1.call-update) | async-done | bytes 8388624 | tf_op jit(solution)/shard_map/all_gather | solution.py:76
  203.6 5.7 %convolution_convert_fusion = bf16[384,4096]{1,0:T(8,128)(2,1)} fusion(bf16[1024,4096]{1,0:T(8,128)(2,1)} %all-gather.5.cloned.1.call-done, s32[]{:T(128)S(6)} %select_n.182, s32[512]{0:T(512)S(1)} %bitcast.56, s32[512]{0:T(512)S(1)} %bitcast.55, s32[512]{0:T(512)S(1)} %add_select_fusion.2, s32[384]{0:T(512)S(1)} %get-tuple-element.29, ...), kind=kOutput, calls=%fused_computation.3 | convolution fusion | flops 1613168640 | bytes 7349252 | tf_op jit(solution)/shard_map/dot_general | solution.py:34
  209.3 4.8 %all-to-all-start.2 = ((bf16[4,96,4096]{2,1,0:T(8,128)(2,1)}), bf16[4,96,4096]{2,1,0:T(8,128)(2,1)}, u32[]{:S(2)}, u32[]{:S(2)}) async-start(bf16[4,96,4096]{2,1,0:T(8,128)(2,1)} %bitcast.52), calls=%async_computation.2 | async-start | bytes 6291456 | tf_op jit(solution)/shard_map/all_to_all | solution.py:102
  214.1 6.5 %fusion.4 = f32[384,768]{1,0:T(8,128)} fusion(bf16[384,4096]{1,0:T(8,128)(2,1)S(1)} %bitcast.49, bf16[4096,384]{1,0:T(8,128)(2,1)} %collective-permute-done.1, bf16[4096,384]{1,0:T(8,128)(2,1)} %bitcast.60), kind=kOutput, calls=%fused_computation.11 | convolution fusion | flops 2428502016 | bytes 10616832 | tf_op jit(solution)/shard_map/dot_general | solution.py:39
  220.6 13.3 %convolution_convert_fusion.3 = bf16[384,4096]{1,0:T(8,128)(2,1)} fusion(bf16[384,4096]{1,0:T(8,128)(2,1)} %collective-permute-done.2, bf16[384,4096]{1,0:T(8,128)(2,1)} %bitcast.63, f32[384,768]{1,0:T(8,128)} %fusion.4, bf16[384,4096]{1,0:T(8,128)(2,1)S(1)} %bitcast.50, bf16[4096,384]{1,0:T(8,128)(2,1)} %collective-permute-done, bf16[4096,384]{1,0:T(8,128)(2,1)} %bitcast.66), kind=kOutput, calls=%fused_computation.6 | convolution fusion | flops 4860346368 | bytes 20054016 | tf_op jit(solution)/shard_map/dot_general | solution.py:41
  233.9 17.0 %all-to-all-done.2 = bf16[4,96,4096]{2,1,0:T(8,128)(2,1)} async-done(((bf16[4,96,4096]{2,1,0:T(8,128)(2,1)}), bf16[4,96,4096]{2,1,0:T(8,128)(2,1)}, u32[]{:S(2)}, u32[]{:S(2)}) %all-to-all-start.2) | async-done | bytes 3145760 | tf_op jit(solution)/shard_map/all_to_all | solution.py:102
  250.9 4.7 %all-to-all-start.1 = ((bf16[16,24,4096]{2,1,0:T(8,128)(2,1)}), bf16[16,24,4096]{2,1,0:T(8,128)(2,1)S(1)}, u32[]{:S(2)}, u32[]{:S(2)}) async-start(bf16[16,24,4096]{2,1,0:T(8,128)(2,1)} %bitcast.53), calls=%async_computation.1 | async-start | bytes 6291456 | tf_op jit(solution)/shard_map/all_to_all | solution.py:104
  255.6 7.4 %fusion.3 = f32[384,768]{1,0:T(8,128)} fusion(bf16[384,4096]{1,0:T(8,128)(2,1)} %bitcast.20, bf16[4096,384]{1,0:T(8,128)(2,1)} %collective-permute-done.1, bf16[4096,384]{1,0:T(8,128)(2,1)} %bitcast.61), kind=kOutput, calls=%fused_computation.10 | convolution fusion | flops 2428502016 | bytes 10616832 | tf_op jit(solution)/shard_map/dot_general | solution.py:39
  263.0 14.2 %convolution_convert_fusion.2 = bf16[384,4096]{1,0:T(8,128)(2,1)} fusion(bf16[384,4096]{1,0:T(8,128)(2,1)} %collective-permute-done.2, bf16[384,4096]{1,0:T(8,128)(2,1)} %bitcast.64, f32[384,768]{1,0:T(8,128)} %fusion.3, bf16[384,4096]{1,0:T(8,128)(2,1)} %bitcast.20, bf16[4096,384]{1,0:T(8,128)(2,1)} %collective-permute-done, bf16[4096,384]{1,0:T(8,128)(2,1)} %bitcast.67), kind=kOutput, calls=%fused_computation.5 | convolution fusion | flops 4860346368 | bytes 20054016 | tf_op jit(solution)/shard_map/dot_general | solution.py:41
  277.2 50.7 %all-to-all-done.1 = bf16[16,24,4096]{2,1,0:T(8,128)(2,1)S(1)} async-done(((bf16[16,24,4096]{2,1,0:T(8,128)(2,1)}), bf16[16,24,4096]{2,1,0:T(8,128)(2,1)S(1)}, u32[]{:S(2)}, u32[]{:S(2)}) %all-to-all-start.1) | async-done | bytes 3145760 | tf_op jit(solution)/shard_map/all_to_all | solution.py:104
  327.9 4.6 %all-to-all-start.3 = ((bf16[16,24,4096]{2,1,0:T(8,128)(2,1)}), bf16[16,24,4096]{2,1,0:T(8,128)(2,1)}, u32[]{:S(2)}, u32[]{:S(2)}) async-start(bf16[16,24,4096]{2,1,0:T(8,128)(2,1)} %bitcast.48), calls=%async_computation.3 | async-start | bytes 6291456 | tf_op jit(solution)/shard_map/all_to_all | solution.py:104
  332.5 0.1 convert_element_type.103
  332.7 0.1 convert_element_type.92
  332.8 0.1 copy.40
  332.9 0.1 copy.41
  333.1 0.1 fusion.42
  333.2 0.8 bitcast_divide_fusion.1
  333.9 0.9 copy.42
  334.8 0.9 copy.51
  335.8 0.1 copy.48
  335.9 0.1 copy.39
  335.9 0.2 select_reduce_fusion.1
  336.1 0.1 select_reduce_fusion
  336.3 3.2 fusion.33
  339.5 65.2 %all-to-all-done.3 = bf16[16,24,4096]{2,1,0:T(8,128)(2,1)} async-done(((bf16[16,24,4096]{2,1,0:T(8,128)(2,1)}), bf16[16,24,4096]{2,1,0:T(8,128)(2,1)}, u32[]{:S(2)}, u32[]{:S(2)}) %all-to-all-start.3) | async-done | bytes 3145760 | tf_op jit(solution)/shard_map/all_to_all | solution.py:104
  404.8 3.3 fusion.37
  408.1 3.6 select_bitcast_fusion
  411.7 1.1 select_bitcast_fusion.1
  (33 shorter events, 0.3 us)
Async XLA Ops:
  7.2 101.2 %all-gather.7.cloned.1.call-start = ((), (), s32[]{:S(2)}) async-start(), calls=%async_computation.5 | async-start | bytes 9437184 | tf_op jit(solution)/shard_map/all_gather | solution.py:76
  7.2 30.9 %copy-start.2 = (s32[1,128,2]{1,2,0:T(2,128)S(1)}, s32[1,128,2]{1,2,0:T(2,128)}, u32[]{:S(2)}) copy-start(s32[1,128,2]{1,2,0:T(2,128)} %param.11) | copy-start | bytes 3076
  7.2 31.0 %copy-start.3 = (s32[1,128,2]{1,2,0:T(2,128)S(1)}, s32[1,128,2]{1,2,0:T(2,128)}, u32[]{:S(2)}) copy-start(s32[1,128,2]{1,2,0:T(2,128)} %param.12) | copy-start | bytes 3076
  9.9 193.7 %all-gather.5.cloned.1.call-start = ((), (), s32[]{:S(2)}) async-start(), calls=%async_computation.4 | async-start | bytes 9437184 | tf_op jit(solution)/shard_map/all_gather | solution.py:76
  10.0 25.5 %collective-permute-start.3 = (bf16[128,4096]{1,0:T(8,128)(2,1)S(1)}, bf16[128,4096]{1,0:T(8,128)(2,1)S(1)}, u32[]{:S(2)}, u32[]{:S(2)}) collective-permute-start(bf16[128,4096]{1,0:T(8,128)(2,1)S(1)} %get-tuple-element.10), channel_id=1, source_target_pairs={{224,32},{32,96},{96,160},{160,224},{64,0},{128,64},{192,128},{0,1... | collective-permute-start | bytes 3145736 | tf_op jit(solution)/shard_map/ppermute | solution.py:73
  35.4 1.0 copy-start.1
  36.4 177.7 %collective-permute-start.1 = (bf16[4096,384]{1,0:T(8,128)(2,1)}, bf16[4096,384]{1,0:T(8,128)(2,1)}, u32[]{:S(2)}, u32[]{:S(2)}) collective-permute-start(bf16[4096,384]{1,0:T(8,128)(2,1)} %bitcast.59), channel_id=1, source_target_pairs={{0,1},{1,0},{2,3},{3,2},{4,5},{5,4},{6,7},{7,6},{8,9},{9,8},{10,11... | collective-permute-start | bytes 9437192 | tf_op jit(solution)/shard_map/ppermute | solution.py:94
  114.0 95.2 %all-to-all-start = ((bf16[4,96,4096]{2,1,0:T(8,128)(2,1)}), bf16[4,96,4096]{2,1,0:T(8,128)(2,1)S(1)}, u32[]{:S(2)}, u32[]{:S(2)}) async-start(bf16[4,96,4096]{2,1,0:T(8,128)(2,1)} %bitcast.51), calls=%async_computation | async-start | bytes 6291456 | tf_op jit(solution)/shard_map/all_to_all | solution.py:102
  118.0 102.6 %collective-permute-start = (bf16[4096,384]{1,0:T(8,128)(2,1)}, bf16[4096,384]{1,0:T(8,128)(2,1)}, u32[]{:S(2)}, u32[]{:S(2)}) collective-permute-start(bf16[4096,384]{1,0:T(8,128)(2,1)} %bitcast.65), channel_id=1, source_target_pairs={{0,1},{1,0},{2,3},{3,2},{4,5},{5,4},{6,7},{7,6},{8,9},{9,8},{10,11... | collective-permute-start | bytes 9437192 | tf_op jit(solution)/shard_map/ppermute | solution.py:93
  119.0 101.6 %collective-permute-start.2 = (bf16[384,4096]{1,0:T(8,128)(2,1)}, bf16[384,4096]{1,0:T(8,128)(2,1)}, u32[]{:S(2)}, u32[]{:S(2)}) collective-permute-start(bf16[384,4096]{1,0:T(8,128)(2,1)} %bitcast.62), channel_id=1, source_target_pairs={{0,1},{1,0},{2,3},{3,2},{4,5},{5,4},{6,7},{7,6},{8,9},{9,8},{10,11... | collective-permute-start | bytes 9437192 | tf_op jit(solution)/shard_map/ppermute | solution.py:95
  209.3 41.7 %all-to-all-start.2 = ((bf16[4,96,4096]{2,1,0:T(8,128)(2,1)}), bf16[4,96,4096]{2,1,0:T(8,128)(2,1)}, u32[]{:S(2)}, u32[]{:S(2)}) async-start(bf16[4,96,4096]{2,1,0:T(8,128)(2,1)} %bitcast.52), calls=%async_computation.2 | async-start | bytes 6291456 | tf_op jit(solution)/shard_map/all_to_all | solution.py:102
  250.9 77.0 %all-to-all-start.1 = ((bf16[16,24,4096]{2,1,0:T(8,128)(2,1)}), bf16[16,24,4096]{2,1,0:T(8,128)(2,1)S(1)}, u32[]{:S(2)}, u32[]{:S(2)}) async-start(bf16[16,24,4096]{2,1,0:T(8,128)(2,1)} %bitcast.53), calls=%async_computation.1 | async-start | bytes 6291456 | tf_op jit(solution)/shard_map/all_to_all | solution.py:104
  327.9 4.9 %copy-start.4 = (f32[1,128,2]{1,2,0:T(2,128)S(1)}, f32[1,128,2]{1,2,0:T(2,128)}, u32[]{:S(2)}) copy-start(f32[1,128,2]{1,2,0:T(2,128)} %param.13) | copy-start | bytes 3076
  327.9 5.0 %copy-start.5 = (f32[1,128,2]{1,2,0:T(2,128)S(1)}, f32[1,128,2]{1,2,0:T(2,128)}, u32[]{:S(2)}) copy-start(f32[1,128,2]{1,2,0:T(2,128)} %param.14) | copy-start | bytes 3076
  327.9 76.9 %all-to-all-start.3 = ((bf16[16,24,4096]{2,1,0:T(8,128)(2,1)}), bf16[16,24,4096]{2,1,0:T(8,128)(2,1)}, u32[]{:S(2)}, u32[]{:S(2)}) async-start(bf16[16,24,4096]{2,1,0:T(8,128)(2,1)} %bitcast.48), calls=%async_computation.3 | async-start | bytes 6291456 | tf_op jit(solution)/shard_map/all_to_all | solution.py:104
  404.8 3.3 copy-start
Sparse Core Ops, SparseCore 0:
  10.4 97.9 all-gather.6
  110.7 92.8 all-gather.4

commit v2 on v1

v2 whole, which is shorter than its diff:
```python
import jax
import jax.numpy as jnp
from jax import lax
from jax.experimental import pallas as pl
from jax.experimental.pallas import tpu as pltpu
from jax.sharding import Mesh
from jax.sharding import PartitionSpec as P

EXPERTS = 16
CAP = 24
X, Z, Y = 4, 4, 4
BF = jnp.bfloat16
F32 = jnp.float32


def slots_of(ids):
    flat = ids.reshape(-1)
    n = flat.shape[0]
    one_hot = (flat[:, None] == jnp.arange(EXPERTS, dtype=jnp.int32)[None, :]).astype(BF)
    place = jnp.arange(n, dtype=jnp.int32)
    below = (place[:, None] > place[None, :]).astype(BF)
    counts = jnp.dot(below, one_hot, preferred_element_type=F32)
    rank = jnp.sum(counts * one_hot.astype(F32), axis=1).astype(jnp.int32)
    return (flat * CAP + rank).reshape(ids.shape)


def outgoing(parts, slots, sources, turn, z_lo):
    t, n = parts[0].shape[0], len(parts)
    row = jnp.arange(X * n * CAP, dtype=jnp.int32)
    block, which, rank = row // (n * CAP), row // CAP % n, row % CAP
    target = ((turn + block) % X * Z + z_lo) * CAP + rank
    held = jnp.arange(n * t, dtype=jnp.int32) // t
    flat = jnp.concatenate([lax.dynamic_index_in_dim(slots, (z_lo - s) % Z, 0, False) for s in sources], axis=0)
    hit = (flat[None, :, 0] == target[:, None]) | (flat[None, :, 1] == target[:, None])
    pick = (hit & (held[None, :] == which[:, None])).astype(BF)
    return jnp.dot(pick, jnp.concatenate(parts, axis=0), preferred_element_type=F32).astype(BF)


def over_x(sent):
    n = sent.shape[0] // X
    blocks = [sent[i * n : (i + 1) * n] for i in range(X)]
    moved = [lax.ppermute(blocks[i], "x", [(j, (j + i) % X) for j in range(X)]) for i in range(1, X)]
    return [blocks[0], *moved]


def place(from_x, source, rank):
    return (from_x * Z + source) * CAP + rank


def to_matrix(to):
    row = jnp.arange(to.shape[0], dtype=jnp.int32)
    return (row[:, None] == to[None, :]).astype(BF)


STEPS = 4


def expert_kernel(n_parts, *refs):
    parts, (order, g0, g1, u0, u1, d0, d1, out, gate, up, hidden) = refs[:n_parts], refs[n_parts:]
    step = pl.program_id(0)

    @pl.when(step == 0)
    def _():
        gate[...] = jnp.zeros_like(gate)
        up[...] = jnp.zeros_like(up)

    @pl.when(step < STEPS)
    def _():
        rows = jnp.concatenate([p[...] for p in parts], axis=0)
        gate[...] += jnp.dot(rows, jnp.concatenate([g0[...], g1[...]], axis=1), preferred_element_type=F32)
        up[...] += jnp.dot(rows, jnp.concatenate([u0[...], u1[...]], axis=1), preferred_element_type=F32)

    @pl.when(step == STEPS - 1)
    def _():
        pre = gate[...]
        value = (pre / (1.0 + jnp.exp(-pre)) * up[...]).astype(BF)
        hidden[...] = jnp.dot(order[...], value, preferred_element_type=F32).astype(BF)

    @pl.when(step >= STEPS)
    def _():
        down = jnp.concatenate([d0[...], d1[...]], axis=0)
        out[...] = jnp.dot(hidden[...], down, preferred_element_type=F32).astype(BF)


def expert(parts, order, gates, ups, downs, flops):
    n, d = order.shape[0], parts[0].shape[1]
    half = gates[0].shape[1]
    cols = d // STEPS

    def first(i):
        return jnp.minimum(i, STEPS - 1)

    def second(i):
        return jnp.maximum(i - STEPS, 0)

    in_specs = [pl.BlockSpec((p.shape[0], cols), lambda i: (0, first(i))) for p in parts]
    in_specs += [pl.BlockSpec((n, n), lambda i: (0, 0))]
    in_specs += [pl.BlockSpec((cols, half), lambda i: (first(i), 0))] * 4
    in_specs += [pl.BlockSpec((half, cols), lambda i: (0, second(i)))] * 2
    return pl.pallas_call(
        lambda *refs: expert_kernel(len(parts), *refs),
        grid=(2 * STEPS,),
        in_specs=in_specs,
        out_specs=pl.BlockSpec((n, cols), lambda i: (0, second(i))),
        out_shape=jax.ShapeDtypeStruct((n, d), BF),
        scratch_shapes=[
            pltpu.VMEM((n, 2 * half), F32),
            pltpu.VMEM((n, 2 * half), F32),
            pltpu.VMEM((n, 2 * half), BF),
        ],
        compiler_params=pltpu.CompilerParams(vmem_limit_bytes=40 * 2**20),
        cost_estimate=pl.CostEstimate(flops=flops, bytes_accessed=10**6, transcendentals=0),
        name="expert",
    )(*parts, order, *gates, *ups, *downs)


def mixing(slots, probs):
    gates = probs / jnp.sum(probs, axis=1, keepdims=True)
    spot = jnp.arange(EXPERTS * CAP, dtype=jnp.int32)
    mix = jnp.sum(
        jnp.where(slots[:, :, None] == spot[None, None, :], gates[:, :, None], 0.0), axis=1
    )
    high = lax.reduce_precision(mix, 8, 7)
    return jnp.concatenate([high, mix - high], axis=0).astype(BF)


def combine(home, back, mix):
    summed = jnp.dot(mix, back, preferred_element_type=F32)
    t = home.shape[0]
    return (home.astype(F32) + (summed[:t] + summed[t:])).astype(BF)


def finish_kernel(upper, home, back, mix, other, out_a, out_b):
    last = combine(home[...], back[...], mix[...])
    swap = upper[0] == 1
    out_a[...] = jnp.where(swap, other[...], last)
    out_b[...] = jnp.where(swap, last, other[...])


def finish(upper, home, back, mix, other):
    t, d = home.shape
    cols = 1024

    def tall(rows):
        return pl.BlockSpec((rows, cols), lambda i: (0, i))

    return pl.pallas_call(
        finish_kernel,
        grid=(d // cols,),
        in_specs=[
            pl.BlockSpec(memory_space=pltpu.SMEM),
            tall(t),
            tall(back.shape[0]),
            pl.BlockSpec(mix.shape, lambda i: (0, 0)),
            tall(t),
        ],
        out_specs=[tall(t), tall(t)],
        out_shape=[jax.ShapeDtypeStruct((t, d), BF)] * 2,
        compiler_params=pltpu.CompilerParams(vmem_limit_bytes=40 * 2**20),
        name="finish",
    )(upper.astype(jnp.int32)[None], home, back, mix, other)


def after(value, *others):
    return lax.optimization_barrier((value, *others))[0]


def shift_ring(block, by):
    n = 2 * Z
    return lax.ppermute(block, ("z_hi", "z_lo"), [(i, (i + by) % n) for i in range(n)])


def body(act_fwd, act_rev, ids_fwd, ids_rev, probs_fwd, probs_rev, w_gate, w_up, w_down):
    x, z_hi, z_lo = lax.axis_index("x"), lax.axis_index("z_hi"), lax.axis_index("z_lo")
    upper = z_hi == 1
    act_fwd, act_rev = act_fwd[0], act_rev[0]

    def choose(a, b):
        return jnp.where(upper, a, b)

    first = choose(act_rev, act_fwd)
    hop = [((y - 1) % Y * 2 + 1, y * 2 + 1) for y in range(Y)]
    hop += [((y + 1) % Y * 2, y * 2) for y in range(Y)]
    second = lax.ppermute(choose(act_fwd, act_rev), ("y", "z_hi"), hop)

    ids = [choose(ids_fwd[0], ids_rev[0]), choose(ids_rev[0], ids_fwd[0])]
    probs = [choose(probs_fwd[0], probs_rev[0]), choose(probs_rev[0], probs_fwd[0])]
    slots = [slots_of(i) for i in ids]
    mine = jnp.stack(slots)
    slots_all = jnp.stack(
        [mine]
        + [lax.ppermute(mine, "z_lo", [(j, (j + i) % Z) for j in range(Z)]) for i in range(1, Z)]
    )

    swap = [(0, 1), (1, 0)]
    gates, ups, downs = ((w[0], lax.ppermute(w[0], "core", swap)) for w in (w_gate, w_up, w_down))

    low = z_lo < 2
    edge = (z_lo == 0) | (z_lo == Z - 1)
    sources = (
        jnp.where(low, 3, 0),
        jnp.where(low, 2, 1),
        jnp.where(low, 0, 3),
        jnp.where(low, 1, 2),
    )
    row = jnp.arange(X * Z * CAP, dtype=jnp.int32)
    group_of, by_x, far, rank = row // (X * 2 * CAP), row // (2 * CAP) % X, row // CAP % 2, row % CAP
    near_far = [jnp.where(far == 0, sources[i], sources[i + 1]) for i in (0, 2)]
    source = jnp.where(group_of == 0, *near_far)
    order_1 = to_matrix(place(by_x, source, rank))
    by_shift, which = row // (Z * CAP), row // CAP % Z
    source = jnp.where(
        which < 2,
        jnp.where(which == 0, sources[0], sources[1]),
        jnp.where(which == 2, sources[2], sources[3]),
    )
    order_2 = to_matrix(place((x - by_shift) % X, source, rank))
    mixes = [mixing(slots[p], probs[p]) for p in range(2)]
    up, down = [first], [first]

    def at(p, same, k):
        a, b = (up, down) if same else (down, up)
        k = [i + 2 * p for i in k]
        return jnp.where(
            low, jnp.where(edge, a[k[0]], a[k[1]]), jnp.where(edge, b[k[0]], b[k[1]])
        )

    def group(p, same):
        if same:
            return [at(p, True, (1, 2)), at(p, True, (2, 3))]
        return [at(p, False, (4, 3)), at(p, False, (5, 4))]

    def all_x(sent):
        return lax.all_to_all(
            sent.reshape(X, -1, sent.shape[1]), "x", split_axis=0, concat_axis=0, tiled=True
        ).reshape(sent.shape)

    def back(done):
        return lax.all_to_all(
            done.reshape(EXPERTS, CAP, -1), ("x", "z_lo"), split_axis=0, concat_axis=0, tiled=True
        ).reshape(done.shape)

    def home(p):
        return jnp.where(low, down[4 + 2 * p], up[4 + 2 * p])

    def hops(step, *beside):
        above, below = up[-1], down[-1]
        if step == 3:
            above, below = jnp.where(low, above, second), jnp.where(low, second, below)
        ends = (shift_ring(above, 1), shift_ring(below, -1))
        ends, beside = lax.optimization_barrier((ends, beside))
        up.append(ends[0])
        down.append(ends[1])
        return beside

    def picked(parts, p, froms, turn):
        return outgoing(parts, slots_all[:, p], froms, turn, z_lo)

    (gates,) = hops(1, gates)
    ups, slots_all = hops(2, ups, slots_all)
    downs, mixes = hops(3, downs, mixes)
    sent_a = picked(group(0, True), 0, sources[:2], 0)
    hops(4, sent_a)
    got_a = all_x(sent_a)
    order_1, order_2 = hops(5, got_a, order_1, order_2)[1:]
    sent_b = picked(group(0, False), 0, sources[2:], 0)
    gates = hops(6, sent_b, gates)[1]
    done_1 = expert([got_a, all_x(sent_b)], order_1, gates, ups, downs, 10**8)
    hops(7, done_1)
    back_1 = back(done_1)
    got_2 = over_x(picked(group(1, True) + group(1, False), 1, sources, x))
    done_2 = expert(got_2, order_2, gates, ups, downs, 2 * 10**11)
    out_1 = combine(home(0), after(back_1, done_2), mixes[0])
    out_a, out_b = finish(upper, home(1), back(done_2), mixes[1], out_1)
    return out_a[None], out_b[None]


def solution(mesh):
    split = Mesh(mesh.devices.reshape(Y, 2, X, Z, 2), ("y", "z_hi", "x", "z_lo", "core"))
    section, spread = ("y", "z_hi"), ("x", "z_lo", "core")
    tokens = P(section, spread, None)
    return jax.shard_map(
        body,
        mesh=split,
        in_specs=(tokens,) * 6 + (P(section, None, spread),) * 2 + (tokens,),
        out_specs=(tokens, tokens),
        check_vma=False,
    )
```

time: 420 us -> 364 us (0.87)
  waiting for transfers between devices: 297 us -> 231 us
  matrix products: 59.7 us -> 8.98 us
  Pallas kernels: 0 us -> 30.8 us
  starting transfers between devices: 24.4 us -> 52.1 us
  other arithmetic: 8.69 us -> 22.2 us
  between operations: 14.3 us -> 0.98 us
  local copies, waits for them, and re-layouts: 4.35 us -> 16.3 us
  blocking collectives: 11.1 us -> 0 us
    ppermute x3 -> x23, waiting for transfers between devices: 0.01 us -> 161 us  [the longest x14 104 us: shift_ring(): lax.ppermute(block, ('z_hi', 'z_lo'), [(i, (i + by) % n) for i in range(n)])]
    all_gather x2 -> x0, waiting for transfers between devices: 142 us -> none  [ring(): full = lax.all_gather(block, ('z_hi', 'z_lo'), axis=0, tiled=True)]
    all_to_all x4, waiting for transfers between devices: 133 us -> 70.4 us  [the longest x2 66.3 us: back(): lax.all_to_all(done.reshape(EXPERTS, CAP, -1), ('x', 'z_lo'), split_axis=...]
    dot_general x8 -> x4, matrix products: 59.3 us -> 8.57 us  [the longest x3 5.43 us: outgoing(): jnp.dot(pick, jnp.concatenate(parts, axis=0), preferred_element_type=F32)]
    pallas_call x0 -> x3, Pallas kernels: none -> 30.8 us  [the longest x2 27.5 us: expert(): pl.pallas_call(lambda *refs: expert_kernel(len(parts), *refs), grid=(2 *...]
    ppermute x3 -> x23, starting transfers between devices: 2.59 us -> 31.3 us  [the longest x14 19.9 us: shift_ring(): lax.ppermute(block, ('z_hi', 'z_lo'), [(i, (i + by) % n) for i in range(n)])]
    ppermute x1, waiting for transfers between devices: 21.8 us -> 0.01 us  [body(): second = lax.ppermute(choose(act_fwd, act_rev), ('y', 'z_hi'), hop)]
    select_n x2 -> x8, other arithmetic: 0.02 us -> 12.8 us  [the longest x3 9.74 us: at(): jnp.where(low, jnp.where(edge, a[k[0]], a[k[1]]), jnp.where(edge, b[k[0]]...]
  transfers between devices with their start and end apart: 10 -> 28, of which waited for: 6 -> 13; matrix products, arithmetic and copies ran while one was open for 15% -> 8% of each run, Pallas kernels for 0% -> 8%
where the time goes in v2:
time: 364 us; the launch traced here: 363 us
  waiting for transfers between devices  231 us (63%)
  starting transfers between devices  52.1 us (14%)
  Pallas kernels  30.8 us (8%)
  other arithmetic  22.2 us (6%)
  local copies, waits for them, and re-layouts  16.3 us (4%)
  matrix products  8.98 us (2%)
    ppermute x14, waiting for transfers between devices, shift_ring(): lax.ppermute(block, ('z_hi', 'z_lo'), [(i, (i + by) % n) for i in range(n)])  104 us
    all_to_all x2, waiting for transfers between devices, back(): lax.all_to_all(done.reshape(EXPERTS, CAP, -1), ('x', 'z_lo'), split_axis=...  66.3 us
    ppermute x3, waiting for transfers between devices, over_x(): lax.ppermute(blocks[i], 'x', [(j, (j + i) % X) for j in range(X)])  56.9 us
    pallas_call x2, Pallas kernels, expert(): pl.pallas_call(lambda *refs: expert_kernel(len(parts), *refs), grid=(2 *...  27.5 us
    ppermute x14, starting transfers between devices, shift_ring(): lax.ppermute(block, ('z_hi', 'z_lo'), [(i, (i + by) % n) for i in range(n)])  19.9 us
    unnamed x40, local copies, waits for them, and re-layouts  13.3 us
    all_to_all x2, starting transfers between devices, back(): lax.all_to_all(done.reshape(EXPERTS, CAP, -1), ('x', 'z_lo'), split_axis=...  10 us
    select_n x3, other arithmetic, at(): jnp.where(low, jnp.where(edge, a[k[0]], a[k[1]]), jnp.where(edge, b[k[0]]...  9.74 us
  transfers between devices with their start and end apart: 28, of which 13 were waited for; matrix products, arithmetic and copies ran while one was open for 8% of the time, Pallas kernels for 8%

profile of v2, /device:TPU:1, one launch (start us, length us, event | category | flops | bytes accessed | tf_op | source)
XLA Modules:
  0.0 362.6 jit_solution(14065440397685034032)
XLA Ops:
  0.7 3.3 collective-permute-start.2
  4.1 3.0 select_bitcast_fusion
  7.1 3.8 %collective-permute-start.1 = (bf16[128,4096]{1,0:T(8,128)(2,1)}, bf16[128,4096]{1,0:T(8,128)(2,1)}, u32[]{:S(2)}, u32[]{:S(2)}) collective-permute-start(bf16[128,4096]{1,0:T(8,128)(2,1)} %get-tuple-element.80), channel_id=1, source_target_pairs={{0,38},{2,0},{4,2},{6,4},{32,6},{34,32},{36,34},{38,36},{1,39},{3,... | collective-permute-start | bytes 3145736 | tf_op jit(solution)/shard_map/ppermute | solution.py:170
  12.3 1.7 collective-permute-start.8
  14.0 20.4 %collective-permute-done = bf16[128,4096]{1,0:T(8,128)(2,1)} collective-permute-done((bf16[128,4096]{1,0:T(8,128)(2,1)}, bf16[128,4096]{1,0:T(8,128)(2,1)}, u32[]{:S(2)}, u32[]{:S(2)}) %collective-permute-start) | collective-permute-done | bytes 1048608 | tf_op jit(solution)/shard_map/ppermute | solution.py:170
  34.4 1.6 collective-permute-start.7
  36.3 2.8 collective-permute-start.9
  39.2 1.8 collective-permute-start.12
  41.0 2.6 collective-permute-start.3
  47.2 20.1 %collective-permute-done.3 = bf16[128,4096]{1,0:T(8,128)(2,1)} collective-permute-done((bf16[128,4096]{1,0:T(8,128)(2,1)}, bf16[128,4096]{1,0:T(8,128)(2,1)}, u32[]{:S(2)}, u32[]{:S(2)}) %collective-permute-start.3) | collective-permute-done | bytes 1048608 | tf_op jit(solution)/shard_map/ppermute | solution.py:170
  67.2 1.7 collective-permute-done.4
  68.9 3.0 broadcast_select_fusion.1
  72.8 1.8 collective-permute-start.11
  76.4 20.4 %collective-permute-done.10 = bf16[128,4096]{1,0:T(8,128)(2,1)S(1)} collective-permute-done((bf16[128,4096]{1,0:T(8,128)(2,1)}, bf16[128,4096]{1,0:T(8,128)(2,1)S(1)}, u32[]{:S(2)}, u32[]{:S(2)}) %collective-permute-start.10) | collective-permute-done | bytes 1048608 | tf_op jit(solution)/shard_map/ppermute | solution.py:170
  97.1 2.4 collective-permute-start.14
  99.5 2.5 select_select_fusion.7
  102.0 1.8 convolution_convert_fusion.2
  103.8 4.0 %all-to-all-start = ((bf16[4,48,4096]{2,1,0:T(8,128)(2,1)}), bf16[4,48,4096]{2,1,0:T(8,128)(2,1)S(1)}, u32[]{:S(2)}, u32[]{:S(2)}) async-start(bf16[4,48,4096]{2,1,0:T(8,128)(2,1)} %bitcast.68), calls=%async_computation | async-start | bytes 3145728 | tf_op jit(solution)/shard_map/all_to_all | solution.py:234
  107.8 12.9 %collective-permute-done.13 = bf16[128,4096]{1,0:T(8,128)(2,1)} collective-permute-done((bf16[128,4096]{1,0:T(8,128)(2,1)S(1)}, bf16[128,4096]{1,0:T(8,128)(2,1)}, u32[]{:S(2)}, u32[]{:S(2)}) %collective-permute-start.13) | collective-permute-done | bytes 1048608 | tf_op jit(solution)/shard_map/ppermute | solution.py:170
  120.7 2.7 collective-permute-start.16
  124.3 1.3 all-to-all-done
  125.6 18.3 %collective-permute-done.15 = bf16[128,4096]{1,0:T(8,128)(2,1)} collective-permute-done((bf16[128,4096]{1,0:T(8,128)(2,1)}, bf16[128,4096]{1,0:T(8,128)(2,1)}, u32[]{:S(2)}, u32[]{:S(2)}) %collective-permute-start.15) | collective-permute-done | bytes 1048608 | tf_op jit(solution)/shard_map/ppermute | solution.py:170
  143.9 2.7 collective-permute-start.18
  146.5 3.7 %select_select_fusion.3 = (bf16[128,4096]{1,0:T(8,128)(2,1)}, bf16[128,4096]{1,0:T(8,128)(2,1)S(1)}, bf16[128,4096]{1,0:T(8,128)(2,1)S(1)}, bf16[128,4096]{1,0:T(8,128)(2,1)}) fusion(bf16[128,4096]{1,0:T(8,128)(2,1)} %collective-permute-done.11, bf16[128,4096]{1,0:T(8,128)(2,1)} %collective-permute-done.14, ...), kind=kLoop, calls=%fused_computation.26 | loop fusion | flops 6291456 | bytes 10485762 | tf_op jit(solution)/shard_map/jit(_where)/select_n | solution.py:224
  150.2 1.8 convolution_convert_fusion.1
  152.0 4.0 %all-to-all-start.1 = ((bf16[4,48,4096]{2,1,0:T(8,128)(2,1)}), bf16[4,48,4096]{2,1,0:T(8,128)(2,1)S(1)}, u32[]{:S(2)}, u32[]{:S(2)}) async-start(bf16[4,48,4096]{2,1,0:T(8,128)(2,1)} %bitcast.67), calls=%async_computation.1 | async-start | bytes 3145728 | tf_op jit(solution)/shard_map/all_to_all | solution.py:234
  156.0 10.1 %collective-permute-done.17 = bf16[128,4096]{1,0:T(8,128)(2,1)} collective-permute-done((bf16[128,4096]{1,0:T(8,128)(2,1)}, bf16[128,4096]{1,0:T(8,128)(2,1)}, u32[]{:S(2)}, u32[]{:S(2)}) %collective-permute-start.17) | collective-permute-done | bytes 1048608 | tf_op jit(solution)/shard_map/ppermute | solution.py:170
  166.1 2.7 collective-permute-start.20
  168.8 2.8 all-to-all-done.1
  171.7 1.9 copy-done.2
  173.5 1.9 copy-done.5
  175.4 14.2 %expert.2 = bf16[384,4096]{1,0:T(8,128)(2,1)} custom-call(bf16[192,4096]{1,0:T(8,128)(2,1)S(1)} %bitcast.55, bf16[192,4096]{1,0:T(8,128)(2,1)S(1)} %bitcast.56, bf16[384,384]{1,0:T(8,128)(2,1)S(1)} %fusion.22.refs_2_, bf16[4096,384]{1,0:T(8,128)(2,1)S(1)} %bitcast.58, bf16[4096,384]{1,0:T(8,128)(2,1)S(1)} %copy-done.5, bf16[4096,384]{1,0:T(8,128)(2,1)} %bitcast.62, ...), custom_call_target="tpu_custom_call" | custom-call | flops 100000000 | bytes 1000000 | tf_op jit(solution)/shard_map/expert/pallas_call | solution.py:100
  189.7 3.6 select_select_fusion.1
  193.3 1.9 convolution_convert_fusion
  195.2 1.7 fusion.97
  197.2 1.9 collective-permute-start.22
  199.7 4.7 %all-to-all-start.3 = ((bf16[16,24,4096]{2,1,0:T(8,128)(2,1)}), bf16[16,24,4096]{2,1,0:T(8,128)(2,1)}, u32[]{:S(2)}, u32[]{:S(2)}) async-start(bf16[16,24,4096]{2,1,0:T(8,128)(2,1)} %bitcast.38), calls=%async_computation.3 | async-start | bytes 6291456 | tf_op jit(solution)/shard_map/all_to_all | solution.py:239
  204.5 17.1 %collective-permute-done.21.refs_1_ = bf16[96,4096]{1,0:T(8,128)(2,1)} collective-permute-done((bf16[96,4096]{1,0:T(8,128)(2,1)}, bf16[96,4096]{1,0:T(8,128)(2,1)}, u32[]{:S(2)}, u32[]{:S(2)}) %collective-permute-start.21) | collective-permute-done | bytes 786464 | tf_op jit(solution)/shard_map/ppermute | solution.py:42
  221.6 27.3 %collective-permute-done.22.refs_2_ = bf16[96,4096]{1,0:T(8,128)(2,1)} collective-permute-done((bf16[96,4096]{1,0:T(8,128)(2,1)}, bf16[96,4096]{1,0:T(8,128)(2,1)}, u32[]{:S(2)}, u32[]{:S(2)}) %collective-permute-start.22) | collective-permute-done | bytes 786464 | tf_op jit(solution)/shard_map/ppermute | solution.py:42
  248.9 12.5 %collective-permute-done.23.refs_3_ = bf16[96,4096]{1,0:T(8,128)(2,1)} collective-permute-done((bf16[96,4096]{1,0:T(8,128)(2,1)}, bf16[96,4096]{1,0:T(8,128)(2,1)}, u32[]{:S(2)}, u32[]{:S(2)}) %collective-permute-start.23) | collective-permute-done | bytes 786464 | tf_op jit(solution)/shard_map/ppermute | solution.py:42
  261.4 1.9 copy-done.6
  264.4 13.3 %expert.3 = bf16[384,4096]{1,0:T(8,128)(2,1)S(1)} custom-call(bf16[96,4096]{1,0:T(8,128)(2,1)S(1)} %copy-done.9, bf16[96,4096]{1,0:T(8,128)(2,1)} %collective-permute-done.21.refs_1_, bf16[96,4096]{1,0:T(8,128)(2,1)} %collective-permute-done.22.refs_2_, bf16[96,4096]{1,0:T(8,128)(2,1)} %collective-permute-done.23.refs_3_, bf16[384,384]{1,0:T(8,128)(2,1)S(1)} %copy-done.10, ...), custom_call_target="tpu_custom_call" | custom-call | flops 199999995904 | bytes 1000000 | tf_op jit(solution)/shard_map/expert/pallas_call | solution.py:100
  277.8 1.6 copy-done.7
  279.4 5.2 %all-to-all-start.2 = ((bf16[16,24,4096]{2,1,0:T(8,128)(2,1)}), bf16[16,24,4096]{2,1,0:T(8,128)(2,1)S(1)}, u32[]{:S(2)}, u32[]{:S(2)}) async-start(bf16[16,24,4096]{2,1,0:T(8,128)(2,1)} %bitcast.60), calls=%async_computation.2 | async-start | bytes 6291456 | tf_op jit(solution)/shard_map/all_to_all | solution.py:239
  284.7 3.1 fusion.100
  287.8 2.7 fusion.8.other
  290.6 66.3 %all-to-all-done.2 = bf16[16,24,4096]{2,1,0:T(8,128)(2,1)S(1)} async-done(((bf16[16,24,4096]{2,1,0:T(8,128)(2,1)}), bf16[16,24,4096]{2,1,0:T(8,128)(2,1)S(1)}, u32[]{:S(2)}, u32[]{:S(2)}) %all-to-all-start.2) | async-done | bytes 3145760 | tf_op jit(solution)/shard_map/all_to_all | solution.py:239
  359.3 3.2 finish.1
  (105 shorter events, 13.7 us)
Async XLA Ops:
  0.6 10.3 %copy-start.16 = (s32[1,128,2]{1,2,0:T(2,128)S(1)}, s32[1,128,2]{1,2,0:T(2,128)}, u32[]{:S(2)}) copy-start(s32[1,128,2]{1,2,0:T(2,128)} %param.11) | copy-start | bytes 3076
  0.6 10.4 %copy-start.17 = (s32[1,128,2]{1,2,0:T(2,128)S(1)}, s32[1,128,2]{1,2,0:T(2,128)}, u32[]{:S(2)}) copy-start(s32[1,128,2]{1,2,0:T(2,128)} %param.12) | copy-start | bytes 3076
  0.7 35.7 %collective-permute-start.2 = (bf16[4096,384]{1,0:T(8,128)(2,1)}, bf16[4096,384]{1,0:T(8,128)(2,1)S(1)}, u32[]{:S(2)}, u32[]{:S(2)}) collective-permute-start(bf16[4096,384]{1,0:T(8,128)(2,1)} %bitcast.57), channel_id=1, source_target_pairs={{0,1},{1,0},{2,3},{3,2},{4,5},{5,4},{6,7},{7,6},{8,9},{9,8},{10,11... | collective-permute-start | bytes 9437192 | tf_op jit(solution)/shard_map/ppermute | solution.py:196
  4.0 43.2 %collective-permute-start.5 = (bf16[4096,384]{1,0:T(8,128)(2,1)}, bf16[4096,384]{1,0:T(8,128)(2,1)}, u32[]{:S(2)}, u32[]{:S(2)}) collective-permute-start(bf16[4096,384]{1,0:T(8,128)(2,1)} %bitcast.61), channel_id=1, source_target_pairs={{0,1},{1,0},{2,3},{3,2},{4,5},{5,4},{6,7},{7,6},{8,9},{9,8},{10,11... | collective-permute-start | bytes 9437192 | tf_op jit(solution)/shard_map/ppermute | solution.py:196
  7.1 27.3 %collective-permute-start = (bf16[128,4096]{1,0:T(8,128)(2,1)}, bf16[128,4096]{1,0:T(8,128)(2,1)}, u32[]{:S(2)}, u32[]{:S(2)}) collective-permute-start(bf16[128,4096]{1,0:T(8,128)(2,1)} %get-tuple-element.80), channel_id=1, source_target_pairs={{0,2},{2,4},{4,6},{6,32},{32,34},{34,36},{36,38},{38,0},{1,3},{3,5... | collective-permute-start | bytes 3145736 | tf_op jit(solution)/shard_map/ppermute | solution.py:170
  7.1 27.3 %collective-permute-start.1 = (bf16[128,4096]{1,0:T(8,128)(2,1)}, bf16[128,4096]{1,0:T(8,128)(2,1)}, u32[]{:S(2)}, u32[]{:S(2)}) collective-permute-start(bf16[128,4096]{1,0:T(8,128)(2,1)} %get-tuple-element.80), channel_id=1, source_target_pairs={{0,38},{2,0},{4,2},{6,4},{32,6},{34,32},{36,34},{38,36},{1,39},{3,... | collective-permute-start | bytes 3145736 | tf_op jit(solution)/shard_map/ppermute | solution.py:170
  12.3 26.8 %collective-permute-start.8 = (s32[2,128,2]{1,2,0:T(2,128)S(1)}, s32[2,128,2]{1,2,0:T(2,128)S(1)}, u32[]{:S(2)}, u32[]{:S(2)}) collective-permute-start(s32[2,128,2]{1,2,0:T(2,128)S(1)} %pad_add_fusion.2), channel_id=1, source_target_pairs={{0,6},{2,0},{4,2},{6,4},{1,7},{3,1},{5,3},{7,5},{8,14},{10,8},{12,... | collective-permute-start | bytes 6152 | tf_op jit(solution)/shard_map/ppermute | solution.py:192
  34.4 6.6 %collective-permute-start.6 = (s32[2,128,2]{1,2,0:T(2,128)S(1)}, s32[2,128,2]{1,2,0:T(2,128)S(1)}, u32[]{:S(2)}, u32[]{:S(2)}) collective-permute-start(s32[2,128,2]{1,2,0:T(2,128)S(1)} %pad_add_fusion.2), channel_id=1, source_target_pairs={{0,2},{2,4},{4,6},{6,0},{1,3},{3,5},{5,7},{7,1},{8,10},{10,12},{12... | collective-permute-start | bytes 6152 | tf_op jit(solution)/shard_map/ppermute | solution.py:192
  34.4 9.2 %collective-permute-start.7 = (s32[2,128,2]{1,2,0:T(2,128)S(1)}, s32[2,128,2]{1,2,0:T(2,128)S(1)}, u32[]{:S(2)}, u32[]{:S(2)}) collective-permute-start(s32[2,128,2]{1,2,0:T(2,128)S(1)} %pad_add_fusion.2), channel_id=1, source_target_pairs={{0,4},{2,6},{4,0},{6,2},{1,5},{3,7},{5,1},{7,3},{8,12},{10,14},{12... | collective-permute-start | bytes 6152 | tf_op jit(solution)/shard_map/ppermute | solution.py:192
  36.3 35.6 %copy-start.4 = (bf16[4096,384]{1,0:T(8,128)(2,1)}, bf16[4096,384]{1,0:T(8,128)(2,1)S(1)}, u32[]{:S(2)}) copy-start(bf16[4096,384]{1,0:T(8,128)(2,1)S(1)} %collective-permute-done.2.refs_4_.refs_6_) | copy-start | bytes 9437188
  36.3 32.6 %collective-permute-start.9 = (bf16[128,4096]{1,0:T(8,128)(2,1)}, bf16[128,4096]{1,0:T(8,128)(2,1)}, u32[]{:S(2)}, u32[]{:S(2)}) collective-permute-start(bf16[128,4096]{1,0:T(8,128)(2,1)} %get-tuple-element.79), channel_id=1, source_target_pairs={{224,32},{32,96},{96,160},{160,224},{64,0},{128,64},{192,128},{0,1... | collective-permute-start | bytes 3145736 | tf_op jit(solution)/shard_map/ppermute | solution.py:184
  39.2 37.2 %collective-permute-start.12 = (bf16[384,4096]{1,0:T(8,128)(2,1)}, bf16[384,4096]{1,0:T(8,128)(2,1)}, u32[]{:S(2)}, u32[]{:S(2)}) collective-permute-start(bf16[384,4096]{1,0:T(8,128)(2,1)} %bitcast.64), channel_id=1, source_target_pairs={{0,1},{1,0},{2,3},{3,2},{4,5},{5,4},{6,7},{7,6},{8,9},{9,8},{10,11... | collective-permute-start | bytes 9437192 | tf_op jit(solution)/shard_map/ppermute | solution.py:196
  41.0 2.6 copy-start.14
  41.0 26.2 %collective-permute-start.3 = (bf16[128,4096]{1,0:T(8,128)(2,1)}, bf16[128,4096]{1,0:T(8,128)(2,1)}, u32[]{:S(2)}, u32[]{:S(2)}) collective-permute-start(bf16[128,4096]{1,0:T(8,128)(2,1)} %collective-permute-done), channel_id=1, source_target_pairs={{0,2},{2,4},{4,6},{6,32},{32,34},{34,36},{36,38},{38,0},{1,3},{3,5... | collective-permute-start | bytes 3145736 | tf_op jit(solution)/shard_map/ppermute | solution.py:170
  43.6 0.6 copy-start.15
  44.2 24.7 %collective-permute-start.4 = (bf16[128,4096]{1,0:T(8,128)(2,1)}, bf16[128,4096]{1,0:T(8,128)(2,1)}, u32[]{:S(2)}, u32[]{:S(2)}) collective-permute-start(bf16[128,4096]{1,0:T(8,128)(2,1)} %collective-permute-done.1), channel_id=1, source_target_pairs={{0,38},{2,0},{4,2},{6,4},{32,6},{34,32},{36,34},{38,36},{1,39},{3,... | collective-permute-start | bytes 3145736 | tf_op jit(solution)/shard_map/ppermute | solution.py:170
  71.9 24.9 %collective-permute-start.10 = (bf16[128,4096]{1,0:T(8,128)(2,1)}, bf16[128,4096]{1,0:T(8,128)(2,1)S(1)}, u32[]{:S(2)}, u32[]{:S(2)}) collective-permute-start(bf16[128,4096]{1,0:T(8,128)(2,1)} %get-tuple-element.82), channel_id=1, source_target_pairs={{0,2},{2,4},{4,6},{6,32},{32,34},{34,36},{36,38},{38,0},{1,3},{3,5... | collective-permute-start | bytes 3145736 | tf_op jit(solution)/shard_map/ppermute | solution.py:170
  72.8 24.0 %collective-permute-start.11 = (bf16[128,4096]{1,0:T(8,128)(2,1)}, bf16[128,4096]{1,0:T(8,128)(2,1)}, u32[]{:S(2)}, u32[]{:S(2)}) collective-permute-start(bf16[128,4096]{1,0:T(8,128)(2,1)} %get-tuple-element.81), channel_id=1, source_target_pairs={{0,38},{2,0},{4,2},{6,4},{32,6},{34,32},{36,34},{38,36},{1,39},{3,... | collective-permute-start | bytes 3145736 | tf_op jit(solution)/shard_map/ppermute | solution.py:170
  96.8 23.9 %collective-permute-start.13 = (bf16[128,4096]{1,0:T(8,128)(2,1)S(1)}, bf16[128,4096]{1,0:T(8,128)(2,1)}, u32[]{:S(2)}, u32[]{:S(2)}) collective-permute-start(bf16[128,4096]{1,0:T(8,128)(2,1)S(1)} %collective-permute-done.10), channel_id=1, source_target_pairs={{0,2},{2,4},{4,6},{6,32},{32,34},{34,36},{36,38},{38,0},{1,3},{3,5... | collective-permute-start | bytes 3145736 | tf_op jit(solution)/shard_map/ppermute | solution.py:170
  97.1 23.6 %collective-permute-start.14 = (bf16[128,4096]{1,0:T(8,128)(2,1)}, bf16[128,4096]{1,0:T(8,128)(2,1)}, u32[]{:S(2)}, u32[]{:S(2)}) collective-permute-start(bf16[128,4096]{1,0:T(8,128)(2,1)} %collective-permute-done.11), channel_id=1, source_target_pairs={{0,38},{2,0},{4,2},{6,4},{32,6},{34,32},{36,34},{38,36},{1,39},{3,... | collective-permute-start | bytes 3145736 | tf_op jit(solution)/shard_map/ppermute | solution.py:170
  103.8 21.8 %all-to-all-start = ((bf16[4,48,4096]{2,1,0:T(8,128)(2,1)}), bf16[4,48,4096]{2,1,0:T(8,128)(2,1)S(1)}, u32[]{:S(2)}, u32[]{:S(2)}) async-start(bf16[4,48,4096]{2,1,0:T(8,128)(2,1)} %bitcast.68), calls=%async_computation | async-start | bytes 3145728 | tf_op jit(solution)/shard_map/all_to_all | solution.py:234
  120.7 23.2 %collective-permute-start.15 = (bf16[128,4096]{1,0:T(8,128)(2,1)}, bf16[128,4096]{1,0:T(8,128)(2,1)}, u32[]{:S(2)}, u32[]{:S(2)}) collective-permute-start(bf16[128,4096]{1,0:T(8,128)(2,1)} %collective-permute-done.13), channel_id=1, source_target_pairs={{0,2},{2,4},{4,6},{6,32},{32,34},{34,36},{36,38},{38,0},{1,3},{3,5... | collective-permute-start | bytes 3145736 | tf_op jit(solution)/shard_map/ppermute | solution.py:170
  120.7 23.2 %collective-permute-start.16 = (bf16[128,4096]{1,0:T(8,128)(2,1)}, bf16[128,4096]{1,0:T(8,128)(2,1)}, u32[]{:S(2)}, u32[]{:S(2)}) collective-permute-start(bf16[128,4096]{1,0:T(8,128)(2,1)} %collective-permute-done.14), channel_id=1, source_target_pairs={{0,38},{2,0},{4,2},{6,4},{32,6},{34,32},{36,34},{38,36},{1,39},{3,... | collective-permute-start | bytes 3145736 | tf_op jit(solution)/shard_map/ppermute | solution.py:170
  143.9 22.2 %collective-permute-start.17 = (bf16[128,4096]{1,0:T(8,128)(2,1)}, bf16[128,4096]{1,0:T(8,128)(2,1)}, u32[]{:S(2)}, u32[]{:S(2)}) collective-permute-start(bf16[128,4096]{1,0:T(8,128)(2,1)} %collective-permute-done.15), channel_id=1, source_target_pairs={{0,2},{2,4},{4,6},{6,32},{32,34},{34,36},{36,38},{38,0},{1,3},{3,5... | collective-permute-start | bytes 3145736 | tf_op jit(solution)/shard_map/ppermute | solution.py:170
  143.9 22.2 %collective-permute-start.18 = (bf16[128,4096]{1,0:T(8,128)(2,1)}, bf16[128,4096]{1,0:T(8,128)(2,1)}, u32[]{:S(2)}, u32[]{:S(2)}) collective-permute-start(bf16[128,4096]{1,0:T(8,128)(2,1)} %collective-permute-done.16), channel_id=1, source_target_pairs={{0,38},{2,0},{4,2},{6,4},{32,6},{34,32},{36,34},{38,36},{1,39},{3,... | collective-permute-start | bytes 3145736 | tf_op jit(solution)/shard_map/ppermute | solution.py:170
  152.0 19.7 %all-to-all-start.1 = ((bf16[4,48,4096]{2,1,0:T(8,128)(2,1)}), bf16[4,48,4096]{2,1,0:T(8,128)(2,1)S(1)}, u32[]{:S(2)}, u32[]{:S(2)}) async-start(bf16[4,48,4096]{2,1,0:T(8,128)(2,1)} %bitcast.67), calls=%async_computation.1 | async-start | bytes 3145728 | tf_op jit(solution)/shard_map/all_to_all | solution.py:234
  166.1 23.6 %collective-permute-start.19 = (bf16[128,4096]{1,0:T(8,128)(2,1)}, bf16[128,4096]{1,0:T(8,128)(2,1)}, u32[]{:S(2)}, u32[]{:S(2)}) collective-permute-start(bf16[128,4096]{1,0:T(8,128)(2,1)} %collective-permute-done.17), channel_id=1, source_target_pairs={{0,2},{2,4},{4,6},{6,32},{32,34},{34,36},{36,38},{38,0},{1,3},{3,5... | collective-permute-start | bytes 3145736 | tf_op jit(solution)/shard_map/ppermute | solution.py:170
  166.1 23.6 %collective-permute-start.20 = (bf16[128,4096]{1,0:T(8,128)(2,1)}, bf16[128,4096]{1,0:T(8,128)(2,1)}, u32[]{:S(2)}, u32[]{:S(2)}) collective-permute-start(bf16[128,4096]{1,0:T(8,128)(2,1)} %collective-permute-done.18), channel_id=1, source_target_pairs={{0,38},{2,0},{4,2},{6,4},{32,6},{34,32},{36,34},{38,36},{1,39},{3,... | collective-permute-start | bytes 3145736 | tf_op jit(solution)/shard_map/ppermute | solution.py:170
  171.6 1.9 copy-start.2
  173.5 1.9 copy-start.5
  189.6 3.6 %copy-start.11 = (bf16[128,4096]{1,0:T(8,128)(2,1)S(1)}, bf16[128,4096]{1,0:T(8,128)(2,1)}, u32[]{:S(2)}) copy-start(bf16[128,4096]{1,0:T(8,128)(2,1)} %get-tuple-element.64) | copy-start | bytes 3145732
  189.6 3.6 %copy-start.12 = (bf16[128,4096]{1,0:T(8,128)(2,1)S(1)}, bf16[128,4096]{1,0:T(8,128)(2,1)}, u32[]{:S(2)}) copy-start(bf16[128,4096]{1,0:T(8,128)(2,1)} %get-tuple-element.73) | copy-start | bytes 3145732
  196.9 24.7 %collective-permute-start.21 = (bf16[96,4096]{1,0:T(8,128)(2,1)}, bf16[96,4096]{1,0:T(8,128)(2,1)}, u32[]{:S(2)}, u32[]{:S(2)}) collective-permute-start(bf16[96,4096]{1,0:T(8,128)(2,1)} %get-tuple-element.70), channel_id=1, source_target_pairs={{0,8},{8,16},{16,24},{24,0},{1,9},{9,17},{17,25},{25,1},{2,10},{10... | collective-permute-start | bytes 2359304 | tf_op jit(solution)/shard_map/ppermute | solution.py:42
  197.2 51.7 %collective-permute-start.22 = (bf16[96,4096]{1,0:T(8,128)(2,1)}, bf16[96,4096]{1,0:T(8,128)(2,1)}, u32[]{:S(2)}, u32[]{:S(2)}) collective-permute-start(bf16[96,4096]{1,0:T(8,128)(2,1)} %get-tuple-element.69), channel_id=1, source_target_pairs={{0,16},{8,24},{16,0},{24,8},{1,17},{9,25},{17,1},{25,9},{2,18},{10... | collective-permute-start | bytes 2359304 | tf_op jit(solution)/shard_map/ppermute | solution.py:42
  199.1 62.4 %collective-permute-start.23 = (bf16[96,4096]{1,0:T(8,128)(2,1)}, bf16[96,4096]{1,0:T(8,128)(2,1)}, u32[]{:S(2)}, u32[]{:S(2)}) collective-permute-start(bf16[96,4096]{1,0:T(8,128)(2,1)} %get-tuple-element.68), channel_id=1, source_target_pairs={{0,24},{8,0},{16,8},{24,16},{1,25},{9,1},{17,9},{25,17},{2,26},{10... | collective-permute-start | bytes 2359304 | tf_op jit(solution)/shard_map/ppermute | solution.py:42
  199.7 61.7 %copy-start.3 = (bf16[1,4096,384]{2,1,0:T(8,128)(2,1)S(1)}, bf16[1,4096,384]{2,1,0:T(8,128)(2,1)}, u32[]{:S(2)}) copy-start(bf16[1,4096,384]{2,1,0:T(8,128)(2,1)} %param.15) | copy-start | bytes 9437188
  199.7 61.7 %copy-start.10 = (bf16[384,384]{1,0:T(8,128)(2,1)S(1)}, bf16[384,384]{1,0:T(8,128)(2,1)}, u32[]{:S(2)}) copy-start(bf16[384,384]{1,0:T(8,128)(2,1)} %fusion.23.refs_4_) | copy-start | bytes 884740
  199.7 79.7 %all-to-all-start.3 = ((bf16[16,24,4096]{2,1,0:T(8,128)(2,1)}), bf16[16,24,4096]{2,1,0:T(8,128)(2,1)}, u32[]{:S(2)}, u32[]{:S(2)}) async-start(bf16[16,24,4096]{2,1,0:T(8,128)(2,1)} %bitcast.38), calls=%async_computation.3 | async-start | bytes 6291456 | tf_op jit(solution)/shard_map/all_to_all | solution.py:239
  261.4 1.9 copy-start.6
  263.3 1.1 copy-start.9
  277.8 1.6 copy-start.7
  279.4 5.3 %copy-start.13 = (bf16[256,384]{1,0:T(8,128)(2,1)S(1)}, bf16[256,384]{1,0:T(8,128)(2,1)}, u32[]{:S(2)}) copy-start(bf16[256,384]{1,0:T(8,128)(2,1)} %pad_maximum_fusion) | copy-start | bytes 589828
  279.4 77.5 %all-to-all-start.2 = ((bf16[16,24,4096]{2,1,0:T(8,128)(2,1)}), bf16[16,24,4096]{2,1,0:T(8,128)(2,1)S(1)}, u32[]{:S(2)}, u32[]{:S(2)}) async-start(bf16[16,24,4096]{2,1,0:T(8,128)(2,1)} %bitcast.60), calls=%async_computation.2 | async-start | bytes 6291456 | tf_op jit(solution)/shard_map/all_to_all | solution.py:239
  287.8 69.1 %copy-start.8 = (bf16[256,384]{1,0:T(8,128)(2,1)S(1)}, bf16[256,384]{1,0:T(8,128)(2,1)}, u32[]{:S(2)}) copy-start(bf16[256,384]{1,0:T(8,128)(2,1)} %pad_maximum_fusion.1.mix) | copy-start | bytes 589828
  356.9 1.2 copy-start
  358.1 1.2 copy-start.1

commit v3 on v2

--- a/solution.py
+++ b/solution.py
@@ -108,7 +108,7 @@
             pltpu.VMEM((n, 2 * half), F32),
             pltpu.VMEM((n, 2 * half), BF),
         ],
-        compiler_params=pltpu.CompilerParams(vmem_limit_bytes=40 * 2**20),
+        compiler_params=pltpu.CompilerParams(vmem_limit_bytes=58 * 2**20),
         cost_estimate=pl.CostEstimate(flops=flops, bytes_accessed=10**6, transcendentals=0),
         name="expert",
     )(*parts, order, *gates, *ups, *downs)
@@ -208,13 +208,7 @@
     near_far = [jnp.where(far == 0, sources[i], sources[i + 1]) for i in (0, 2)]
     source = jnp.where(group_of == 0, *near_far)
     order_1 = to_matrix(place(by_x, source, rank))
-    by_shift, which = row // (Z * CAP), row // CAP % Z
-    source = jnp.where(
-        which < 2,
-        jnp.where(which == 0, sources[0], sources[1]),
-        jnp.where(which == 2, sources[2], sources[3]),
-    )
-    order_2 = to_matrix(place((x - by_shift) % X, source, rank))
+    order_2 = to_matrix(place(jnp.where(group_of == 0, by_x, (x - by_x) % X), source, rank))
     mixes = [mixing(slots[p], probs[p]) for p in range(2)]
     up, down = [first], [first]
 
@@ -257,19 +251,21 @@
         return outgoing(parts, slots_all[:, p], froms, turn, z_lo)
 
     (gates,) = hops(1, gates)
-    ups, slots_all = hops(2, ups, slots_all)
-    downs, mixes = hops(3, downs, mixes)
+    (ups,) = hops(2, ups)
+    downs, mixes, slots_all = hops(3, downs, mixes, slots_all)
     sent_a = picked(group(0, True), 0, sources[:2], 0)
     hops(4, sent_a)
     got_a = all_x(sent_a)
     order_1, order_2 = hops(5, got_a, order_1, order_2)[1:]
     sent_b = picked(group(0, False), 0, sources[2:], 0)
     gates = hops(6, sent_b, gates)[1]
-    done_1 = expert([got_a, all_x(sent_b)], order_1, gates, ups, downs, 10**8)
+    got_b = all_x(sent_b)
+    done_1 = expert([got_a, got_b], order_1, gates, ups, downs, 10**8)
     hops(7, done_1)
-    back_1 = back(done_1)
-    got_2 = over_x(picked(group(1, True) + group(1, False), 1, sources, x))
-    done_2 = expert(got_2, order_2, gates, ups, downs, 2 * 10**11)
+    got_a2 = all_x(after(picked(group(1, True), 1, sources[:2], 0), got_b))
+    back_1 = back(after(done_1, got_a2))
+    got_b2 = over_x(picked(group(1, False), 1, sources[2:], x))
+    done_2 = expert([got_a2, *got_b2], order_2, gates, ups, downs, 2 * 10**11)
     out_1 = combine(home(0), after(back_1, done_2), mixes[0])
     out_a, out_b = finish(upper, home(1), back(done_2), mixes[1], out_1)
     return out_a[None], out_b[None]

time: 364 us -> 356 us (0.978)
  waiting for transfers between devices: 231 us -> 222 us
  local copies, waits for them, and re-layouts: 16.3 us -> 9.52 us
  Pallas kernels: 30.8 us -> 35.9 us
    ppermute x3, waiting for transfers between devices: 56.9 us -> 3.77 us  [over_x(): lax.ppermute(blocks[i], 'x', [(j, (j + i) % X) for j in range(X)])]
    all_to_all x2, waiting for transfers between devices: 66.3 us -> 118 us  [back(): lax.all_to_all(done.reshape(EXPERTS, CAP, -1), ('x', 'z_lo'), split_axis=...]
    ppermute x14, waiting for transfers between devices: 104 us -> 81.8 us  [shift_ring(): lax.ppermute(block, ('z_hi', 'z_lo'), [(i, (i + by) % n) for i in range(n)])]
    ppermute x3, waiting for transfers between devices: 0.01 us -> 17.5 us  [body(): lax.ppermute(mine, 'z_lo', [(j, (j + i) % Z) for j in range(Z)])]
    unnamed x40 -> x30, local copies, waits for them, and re-layouts: 13.3 us -> 5.74 us
    pallas_call x2, Pallas kernels: 27.5 us -> 32.6 us  [expert(): pl.pallas_call(lambda *refs: expert_kernel(len(parts), *refs), grid=(2 *...]
    all_to_all x2 -> x3, starting transfers between devices: 8.03 us -> 12.2 us  [all_x(): lax.all_to_all(sent.reshape(X, -1, sent.shape[1]), 'x', split_axis=0, con...]
    all_to_all x2 -> x3, waiting for transfers between devices: 4.08 us -> 0.01 us  [all_x(): lax.all_to_all(sent.reshape(X, -1, sent.shape[1]), 'x', split_axis=0, con...]
  transfers between devices with their start and end apart: 28 -> 29, of which waited for: 13 -> 11; matrix products, arithmetic and copies ran while one was open for 8% -> 10% of each run, Pallas kernels for 8% -> 9%
where the time goes in v3:
time: 356 us; the launch traced here: 355 us
  waiting for transfers between devices  222 us (62%)
  starting transfers between devices  55.7 us (16%)
  Pallas kernels  35.9 us (10%)
  other arithmetic  20.7 us (6%)
  matrix products  10.7 us (3%)
  local copies, waits for them, and re-layouts  9.52 us (3%)
    all_to_all x2, waiting for transfers between devices, back(): lax.all_to_all(done.reshape(EXPERTS, CAP, -1), ('x', 'z_lo'), split_axis=...  118 us
    ppermute x14, waiting for transfers between devices, shift_ring(): lax.ppermute(block, ('z_hi', 'z_lo'), [(i, (i + by) % n) for i in range(n)])  81.8 us
    pallas_call x2, Pallas kernels, expert(): pl.pallas_call(lambda *refs: expert_kernel(len(parts), *refs), grid=(2 *...  32.6 us
    ppermute x14, starting transfers between devices, shift_ring(): lax.ppermute(block, ('z_hi', 'z_lo'), [(i, (i + by) % n) for i in range(n)])  19.9 us
    ppermute x3, waiting for transfers between devices, body(): lax.ppermute(mine, 'z_lo', [(j, (j + i) % Z) for j in range(Z)])  17.5 us
    all_to_all x3, starting transfers between devices, all_x(): lax.all_to_all(sent.reshape(X, -1, sent.shape[1]), 'x', split_axis=0, con...  12.2 us
    select_n x3, other arithmetic, at(): jnp.where(low, jnp.where(edge, a[k[0]], a[k[1]]), jnp.where(edge, b[k[0]]...  8.97 us
    all_to_all x2, starting transfers between devices, back(): lax.all_to_all(done.reshape(EXPERTS, CAP, -1), ('x', 'z_lo'), split_axis=...  8.38 us
  transfers between devices with their start and end apart: 29, of which 11 were waited for; matrix products, arithmetic and copies ran while one was open for 10% of the time, Pallas kernels for 9%

profile of v3, /device:TPU:1, one launch (start us, length us, event | category | flops | bytes accessed | tf_op | source)
XLA Modules:
  0.0 355.1 jit_solution(12780721414559920311)
XLA Ops:
  0.6 3.3 collective-permute-start.2
  4.1 2.7 select_bitcast_fusion
  6.8 3.8 %collective-permute-start.1 = (bf16[128,4096]{1,0:T(8,128)(2,1)S(1)}, bf16[128,4096]{1,0:T(8,128)(2,1)S(1)}, u32[]{:S(2)}, u32[]{:S(2)}) collective-permute-start(bf16[128,4096]{1,0:T(8,128)(2,1)S(1)} %get-tuple-element.80), channel_id=1, source_target_pairs={{0,38},{2,0},{4,2},{6,4},{32,6},{34,32},{36,34},{38,36},{1,39},{3,... | collective-permute-start | bytes 3145736 | tf_op jit(solution)/shard_map/ppermute | solution.py:170
  10.6 2.7 collective-permute-start.6
  14.9 18.9 %collective-permute-done = bf16[128,4096]{1,0:T(8,128)(2,1)S(1)} collective-permute-done((bf16[128,4096]{1,0:T(8,128)(2,1)S(1)}, bf16[128,4096]{1,0:T(8,128)(2,1)S(1)}, u32[]{:S(2)}, u32[]{:S(2)}) %collective-permute-start) | collective-permute-done | bytes 1048608 | tf_op jit(solution)/shard_map/ppermute | solution.py:170
  34.7 1.0 copy-done.6
  35.7 2.7 collective-permute-start.4
  42.6 19.0 %collective-permute-done.3 = bf16[128,4096]{1,0:T(8,128)(2,1)S(1)} collective-permute-done((bf16[128,4096]{1,0:T(8,128)(2,1)S(1)}, bf16[128,4096]{1,0:T(8,128)(2,1)S(1)}, u32[]{:S(2)}, u32[]{:S(2)}) %collective-permute-start.3) | collective-permute-done | bytes 1048608 | tf_op jit(solution)/shard_map/ppermute | solution.py:170
  61.7 2.7 broadcast_select_fusion.1
  64.4 1.2 collective-permute-start.7
  65.5 1.5 collective-permute-start.8
  68.0 3.0 collective-permute-start.12
  71.1 17.5 %collective-permute-done.12 = s32[2,128,2]{1,2,0:T(2,128)S(1)} collective-permute-done((s32[2,128,2]{1,2,0:T(2,128)S(1)}, s32[2,128,2]{1,2,0:T(2,128)S(1)}, u32[]{:S(2)}, u32[]{:S(2)}) %collective-permute-start.12) | collective-permute-done | bytes 2080 | tf_op jit(solution)/shard_map/ppermute | solution.py:192
  88.6 1.1 collective-permute-done.7
  89.7 2.0 collective-permute-start.13
  92.4 1.8 select_select_fusion.7
  94.2 1.8 convolution_convert_fusion.3
  96.0 4.0 %all-to-all-start = ((bf16[4,48,4096]{2,1,0:T(8,128)(2,1)}), bf16[4,48,4096]{2,1,0:T(8,128)(2,1)S(1)}, u32[]{:S(2)}, u32[]{:S(2)}) async-start(bf16[4,48,4096]{2,1,0:T(8,128)(2,1)} %bitcast.70), calls=%async_computation | async-start | bytes 3145728 | tf_op jit(solution)/shard_map/all_to_all | solution.py:228
  100.0 13.7 %collective-permute-done.13 = bf16[128,4096]{1,0:T(8,128)(2,1)} collective-permute-done((bf16[128,4096]{1,0:T(8,128)(2,1)S(1)}, bf16[128,4096]{1,0:T(8,128)(2,1)}, u32[]{:S(2)}, u32[]{:S(2)}) %collective-permute-start.13) | collective-permute-done | bytes 1048608 | tf_op jit(solution)/shard_map/ppermute | solution.py:170
  115.2 1.8 collective-permute-start.16
  118.6 18.7 %collective-permute-done.15 = bf16[128,4096]{1,0:T(8,128)(2,1)} collective-permute-done((bf16[128,4096]{1,0:T(8,128)(2,1)}, bf16[128,4096]{1,0:T(8,128)(2,1)}, u32[]{:S(2)}, u32[]{:S(2)}) %collective-permute-start.15) | collective-permute-done | bytes 1048608 | tf_op jit(solution)/shard_map/ppermute | solution.py:170
  137.3 1.2 collective-permute-start.17
  138.5 1.4 collective-permute-start.18
  139.9 3.7 %select_select_fusion.3 = (bf16[128,4096]{1,0:T(8,128)(2,1)}, bf16[128,4096]{1,0:T(8,128)(2,1)S(1)}, bf16[128,4096]{1,0:T(8,128)(2,1)S(1)}, bf16[128,4096]{1,0:T(8,128)(2,1)}) fusion(bf16[128,4096]{1,0:T(8,128)(2,1)} %collective-permute-done.8, bf16[128,4096]{1,0:T(8,128)(2,1)} %collective-permute-done.14, bf16[128,4096]{1,0:T(8,128)(2,1)S(1)} %collective-permute-done.7, ...), kind=kLoop, calls=%fused_computation.26 | loop fusion | flops 6291456 | bytes 10485762 | tf_op jit(solution)/shard_map/jit(_where)/select_n | solution.py:218
  143.6 1.8 convolution_convert_fusion.2
  145.4 4.1 %all-to-all-start.1 = ((bf16[4,48,4096]{2,1,0:T(8,128)(2,1)}), bf16[4,48,4096]{2,1,0:T(8,128)(2,1)S(1)}, u32[]{:S(2)}, u32[]{:S(2)}) async-start(bf16[4,48,4096]{2,1,0:T(8,128)(2,1)} %bitcast.32), calls=%async_computation.1 | async-start | bytes 3145728 | tf_op jit(solution)/shard_map/all_to_all | solution.py:228
  149.5 9.8 %collective-permute-done.17 = bf16[128,4096]{1,0:T(8,128)(2,1)} collective-permute-done((bf16[128,4096]{1,0:T(8,128)(2,1)}, bf16[128,4096]{1,0:T(8,128)(2,1)}, u32[]{:S(2)}, u32[]{:S(2)}) %collective-permute-start.17) | collective-permute-done | bytes 1048608 | tf_op jit(solution)/shard_map/ppermute | solution.py:170
  159.3 1.1 collective-permute-start.19
  160.4 1.6 collective-permute-start.20
  162.0 3.0 convolution_convert_fusion.1
  165.0 4.0 %all-to-all-start.2 = ((bf16[4,48,4096]{2,1,0:T(8,128)(2,1)}), bf16[4,48,4096]{2,1,0:T(8,128)(2,1)S(1)}, u32[]{:S(2)}, u32[]{:S(2)}) async-start(bf16[4,48,4096]{2,1,0:T(8,128)(2,1)} %bitcast.69), calls=%async_computation.2 | async-start | bytes 3145728 | tf_op jit(solution)/shard_map/all_to_all | solution.py:228
  169.1 16.3 %expert.2 = bf16[384,4096]{1,0:T(8,128)(2,1)} custom-call(bf16[192,4096]{1,0:T(8,128)(2,1)} %bitcast.59, bf16[192,4096]{1,0:T(8,128)(2,1)} %bitcast.60, bf16[384,384]{1,0:T(8,128)(2,1)} %fusion.16.refs_2_, bf16[4096,384]{1,0:T(8,128)(2,1)} %bitcast.62, bf16[4096,384]{1,0:T(8,128)(2,1)} %collective-permute-done.2.refs_4_.refs_7_, bf16[4096,384]{1,0:T(8,128)(2,1)} %bitcast.65, ...), custom_call_target="tpu_custom_call" | custom-call | flops 100000000 | bytes 1000000 | tf_op jit(solution)/shard_map/expert/pallas_call | solution.py:100
  185.4 3.5 select_select_fusion.1
  190.3 1.5 collective-permute-start.21
  191.8 2.4 collective-permute-start.22
  194.2 1.2 collective-permute-start.23
  195.4 1.2 copy-done.4
  196.5 4.5 %all-to-all-start.4 = ((bf16[16,24,4096]{2,1,0:T(8,128)(2,1)}), bf16[16,24,4096]{2,1,0:T(8,128)(2,1)}, u32[]{:S(2)}, u32[]{:S(2)}) async-start(bf16[16,24,4096]{2,1,0:T(8,128)(2,1)} %bitcast.42), calls=%async_computation.4 | async-start | bytes 6291456 | tf_op jit(solution)/shard_map/all_to_all | solution.py:233
  201.0 3.8 %collective-permute-done.22.refs_3_ = bf16[48,4096]{1,0:T(8,128)(2,1)} collective-permute-done((bf16[48,4096]{1,0:T(8,128)(2,1)S(1)}, bf16[48,4096]{1,0:T(8,128)(2,1)}, u32[]{:S(2)}, u32[]{:S(2)}) %collective-permute-start.22) | collective-permute-done | bytes 393248 | tf_op jit(solution)/shard_map/ppermute | solution.py:42
  204.8 16.3 %expert.3 = bf16[384,4096]{1,0:T(8,128)(2,1)} custom-call(bf16[192,4096]{1,0:T(8,128)(2,1)} %bitcast.68, bf16[48,4096]{1,0:T(8,128)(2,1)} %get-tuple-element.84.refs_1_, bf16[48,4096]{1,0:T(8,128)(2,1)} %copy-done.12, bf16[48,4096]{1,0:T(8,128)(2,1)} %collective-permute-done.22.refs_3_, bf16[48,4096]{1,0:T(8,128)(2,1)} %collective-permute-done.23.refs_4_, ...), custom_call_target="tpu_custom_call" | custom-call | flops 199999995904 | bytes 1000000 | tf_op jit(solution)/shard_map/expert/pallas_call | solution.py:100
  221.2 52.1 %all-to-all-done.4 = bf16[16,24,4096]{2,1,0:T(8,128)(2,1)} async-done(((bf16[16,24,4096]{2,1,0:T(8,128)(2,1)}), bf16[16,24,4096]{2,1,0:T(8,128)(2,1)}, u32[]{:S(2)}, u32[]{:S(2)}) %all-to-all-start.4) | async-done | bytes 3145760 | tf_op jit(solution)/shard_map/all_to_all | solution.py:233
  273.3 3.9 %all-to-all-start.3 = ((bf16[16,24,4096]{2,1,0:T(8,128)(2,1)}), bf16[16,24,4096]{2,1,0:T(8,128)(2,1)S(1)}, u32[]{:S(2)}, u32[]{:S(2)}) async-start(bf16[16,24,4096]{2,1,0:T(8,128)(2,1)} %bitcast.67), calls=%async_computation.3 | async-start | bytes 6291456 | tf_op jit(solution)/shard_map/all_to_all | solution.py:233
  277.2 3.1 fusion.100
  280.3 2.7 fusion.1.other
  283.0 66.3 %all-to-all-done.3 = bf16[16,24,4096]{2,1,0:T(8,128)(2,1)S(1)} async-done(((bf16[16,24,4096]{2,1,0:T(8,128)(2,1)}), bf16[16,24,4096]{2,1,0:T(8,128)(2,1)S(1)}, u32[]{:S(2)}, u32[]{:S(2)}) %all-to-all-start.3) | async-done | bytes 3145760 | tf_op jit(solution)/shard_map/all_to_all | solution.py:233
  349.4 1.2 copy-done
  350.6 1.2 copy-done.1
  351.8 3.2 finish.1
  (97 shorter events, 13.0 us)
Async XLA Ops:
  0.6 35.1 %collective-permute-start.2 = (bf16[4096,384]{1,0:T(8,128)(2,1)}, bf16[4096,384]{1,0:T(8,128)(2,1)}, u32[]{:S(2)}, u32[]{:S(2)}) collective-permute-start(bf16[4096,384]{1,0:T(8,128)(2,1)} %bitcast.61), channel_id=1, source_target_pairs={{0,1},{1,0},{2,3},{3,2},{4,5},{5,4},{6,7},{7,6},{8,9},{9,8},{10,11... | collective-permute-start | bytes 9437192 | tf_op jit(solution)/shard_map/ppermute | solution.py:196
  4.0 38.6 %collective-permute-start.5 = (bf16[4096,384]{1,0:T(8,128)(2,1)}, bf16[4096,384]{1,0:T(8,128)(2,1)}, u32[]{:S(2)}, u32[]{:S(2)}) collective-permute-start(bf16[4096,384]{1,0:T(8,128)(2,1)} %bitcast.64), channel_id=1, source_target_pairs={{0,1},{1,0},{2,3},{3,2},{4,5},{5,4},{6,7},{7,6},{8,9},{9,8},{10,11... | collective-permute-start | bytes 9437192 | tf_op jit(solution)/shard_map/ppermute | solution.py:196
  4.1 9.3 %copy-start.9 = (s32[1,128,2]{1,2,0:T(2,128)S(1)}, s32[1,128,2]{1,2,0:T(2,128)}, u32[]{:S(2)}) copy-start(s32[1,128,2]{1,2,0:T(2,128)} %param.11) | copy-start | bytes 3076
  4.1 9.4 %copy-start.10 = (s32[1,128,2]{1,2,0:T(2,128)S(1)}, s32[1,128,2]{1,2,0:T(2,128)}, u32[]{:S(2)}) copy-start(s32[1,128,2]{1,2,0:T(2,128)} %param.12) | copy-start | bytes 3076
  4.1 36.9 %copy-start.11 = (f32[1,128,2]{1,2,0:T(2,128)S(1)}, f32[1,128,2]{1,2,0:T(2,128)}, u32[]{:S(2)}) copy-start(f32[1,128,2]{1,2,0:T(2,128)} %param.13) | copy-start | bytes 3076
  6.8 27.0 %collective-permute-start = (bf16[128,4096]{1,0:T(8,128)(2,1)S(1)}, bf16[128,4096]{1,0:T(8,128)(2,1)S(1)}, u32[]{:S(2)}, u32[]{:S(2)}) collective-permute-start(bf16[128,4096]{1,0:T(8,128)(2,1)S(1)} %get-tuple-element.80), channel_id=1, source_target_pairs={{0,2},{2,4},{4,6},{6,32},{32,34},{34,36},{36,38},{38,0},{1,3},{3,5... | collective-permute-start | bytes 3145736 | tf_op jit(solution)/shard_map/ppermute | solution.py:170
  6.8 28.0 %collective-permute-start.1 = (bf16[128,4096]{1,0:T(8,128)(2,1)S(1)}, bf16[128,4096]{1,0:T(8,128)(2,1)S(1)}, u32[]{:S(2)}, u32[]{:S(2)}) collective-permute-start(bf16[128,4096]{1,0:T(8,128)(2,1)S(1)} %get-tuple-element.80), channel_id=1, source_target_pairs={{0,38},{2,0},{4,2},{6,4},{32,6},{34,32},{36,34},{38,36},{1,39},{3,... | collective-permute-start | bytes 3145736 | tf_op jit(solution)/shard_map/ppermute | solution.py:170
  10.6 51.1 %collective-permute-start.6 = (bf16[128,4096]{1,0:T(8,128)(2,1)}, bf16[128,4096]{1,0:T(8,128)(2,1)}, u32[]{:S(2)}, u32[]{:S(2)}) collective-permute-start(bf16[128,4096]{1,0:T(8,128)(2,1)} %get-tuple-element.79), channel_id=1, source_target_pairs={{224,32},{32,96},{96,160},{160,224},{64,0},{128,64},{192,128},{0,1... | collective-permute-start | bytes 3145736 | tf_op jit(solution)/shard_map/ppermute | solution.py:184
  33.8 30.6 %copy-start.5 = (bf16[128,4096]{1,0:T(8,128)(2,1)}, bf16[128,4096]{1,0:T(8,128)(2,1)S(1)}, u32[]{:S(2)}) copy-start(bf16[128,4096]{1,0:T(8,128)(2,1)S(1)} %collective-permute-done) | copy-start | bytes 3145732
  33.8 54.8 %collective-permute-start.9 = (bf16[384,4096]{1,0:T(8,128)(2,1)}, bf16[384,4096]{1,0:T(8,128)(2,1)}, u32[]{:S(2)}, u32[]{:S(2)}) collective-permute-start(bf16[384,4096]{1,0:T(8,128)(2,1)} %bitcast.5.refs_7_.refs_10_), channel_id=1, source_target_pairs={{0,1},{1,0},{2,3},{3,2},{4,5},{5,4},{6,7},{7,6},{8,9},{9,8},{10,11... | collective-permute-start | bytes 9437192 | tf_op jit(solution)/shard_map/ppermute | solution.py:196
  34.7 1.0 copy-start.6
  35.7 26.0 %collective-permute-start.3 = (bf16[128,4096]{1,0:T(8,128)(2,1)S(1)}, bf16[128,4096]{1,0:T(8,128)(2,1)S(1)}, u32[]{:S(2)}, u32[]{:S(2)}) collective-permute-start(bf16[128,4096]{1,0:T(8,128)(2,1)S(1)} %collective-permute-done), channel_id=1, source_target_pairs={{0,2},{2,4},{4,6},{6,32},{32,34},{34,36},{36,38},{38,0},{1,3},{3,5... | collective-permute-start | bytes 3145736 | tf_op jit(solution)/shard_map/ppermute | solution.py:170
  35.7 26.0 %collective-permute-start.4 = (bf16[128,4096]{1,0:T(8,128)(2,1)}, bf16[128,4096]{1,0:T(8,128)(2,1)S(1)}, u32[]{:S(2)}, u32[]{:S(2)}) collective-permute-start(bf16[128,4096]{1,0:T(8,128)(2,1)} %copy-done.6), channel_id=1, source_target_pairs={{0,38},{2,0},{4,2},{6,4},{32,6},{34,32},{36,34},{38,36},{1,39},{3,... | collective-permute-start | bytes 3145736 | tf_op jit(solution)/shard_map/ppermute | solution.py:170
  42.5 25.5 %collective-permute-start.10 = (s32[2,128,2]{1,2,0:T(2,128)S(1)}, s32[2,128,2]{1,2,0:T(2,128)S(1)}, u32[]{:S(2)}, u32[]{:S(2)}) collective-permute-start(s32[2,128,2]{1,2,0:T(2,128)S(1)} %pad_add_fusion.1), channel_id=1, source_target_pairs={{0,2},{2,4},{4,6},{6,0},{1,3},{3,5},{5,7},{7,1},{8,10},{10,12},{12... | collective-permute-start | bytes 6152 | tf_op jit(solution)/shard_map/ppermute | solution.py:192
  61.7 9.4 %collective-permute-start.11 = (s32[2,128,2]{1,2,0:T(2,128)S(1)}, s32[2,128,2]{1,2,0:T(2,128)S(1)}, u32[]{:S(2)}, u32[]{:S(2)}) collective-permute-start(s32[2,128,2]{1,2,0:T(2,128)S(1)} %pad_add_fusion.1), channel_id=1, source_target_pairs={{0,4},{2,6},{4,0},{6,2},{1,5},{3,7},{5,1},{7,3},{8,12},{10,14},{12... | collective-permute-start | bytes 6152 | tf_op jit(solution)/shard_map/ppermute | solution.py:192
  64.4 25.3 %collective-permute-start.7 = (bf16[128,4096]{1,0:T(8,128)(2,1)}, bf16[128,4096]{1,0:T(8,128)(2,1)S(1)}, u32[]{:S(2)}, u32[]{:S(2)}) collective-permute-start(bf16[128,4096]{1,0:T(8,128)(2,1)} %get-tuple-element.86), channel_id=1, source_target_pairs={{0,2},{2,4},{4,6},{6,32},{32,34},{34,36},{36,38},{38,0},{1,3},{3,5... | collective-permute-start | bytes 3145736 | tf_op jit(solution)/shard_map/ppermute | solution.py:170
  65.5 24.1 %collective-permute-start.8 = (bf16[128,4096]{1,0:T(8,128)(2,1)}, bf16[128,4096]{1,0:T(8,128)(2,1)}, u32[]{:S(2)}, u32[]{:S(2)}) collective-permute-start(bf16[128,4096]{1,0:T(8,128)(2,1)} %get-tuple-element.85), channel_id=1, source_target_pairs={{0,38},{2,0},{4,2},{6,4},{32,6},{34,32},{36,34},{38,36},{1,39},{3,... | collective-permute-start | bytes 3145736 | tf_op jit(solution)/shard_map/ppermute | solution.py:170
  68.0 20.5 %collective-permute-start.12 = (s32[2,128,2]{1,2,0:T(2,128)S(1)}, s32[2,128,2]{1,2,0:T(2,128)S(1)}, u32[]{:S(2)}, u32[]{:S(2)}) collective-permute-start(s32[2,128,2]{1,2,0:T(2,128)S(1)} %pad_add_fusion.1), channel_id=1, source_target_pairs={{0,6},{2,0},{4,2},{6,4},{1,7},{3,1},{5,3},{7,5},{8,14},{10,8},{12,... | collective-permute-start | bytes 6152 | tf_op jit(solution)/shard_map/ppermute | solution.py:192
  89.7 24.0 %collective-permute-start.13 = (bf16[128,4096]{1,0:T(8,128)(2,1)S(1)}, bf16[128,4096]{1,0:T(8,128)(2,1)}, u32[]{:S(2)}, u32[]{:S(2)}) collective-permute-start(bf16[128,4096]{1,0:T(8,128)(2,1)S(1)} %collective-permute-done.7), channel_id=1, source_target_pairs={{0,2},{2,4},{4,6},{6,32},{32,34},{34,36},{36,38},{38,0},{1,3},{3,5... | collective-permute-start | bytes 3145736 | tf_op jit(solution)/shard_map/ppermute | solution.py:170
  91.7 22.7 %collective-permute-start.14 = (bf16[128,4096]{1,0:T(8,128)(2,1)}, bf16[128,4096]{1,0:T(8,128)(2,1)}, u32[]{:S(2)}, u32[]{:S(2)}) collective-permute-start(bf16[128,4096]{1,0:T(8,128)(2,1)} %collective-permute-done.8), channel_id=1, source_target_pairs={{0,38},{2,0},{4,2},{6,4},{32,6},{34,32},{36,34},{38,36},{1,39},{3,... | collective-permute-start | bytes 3145736 | tf_op jit(solution)/shard_map/ppermute | solution.py:170
  96.0 22.6 %all-to-all-start = ((bf16[4,48,4096]{2,1,0:T(8,128)(2,1)}), bf16[4,48,4096]{2,1,0:T(8,128)(2,1)S(1)}, u32[]{:S(2)}, u32[]{:S(2)}) async-start(bf16[4,48,4096]{2,1,0:T(8,128)(2,1)} %bitcast.70), calls=%async_computation | async-start | bytes 3145728 | tf_op jit(solution)/shard_map/all_to_all | solution.py:228
  114.3 22.9 %collective-permute-start.15 = (bf16[128,4096]{1,0:T(8,128)(2,1)}, bf16[128,4096]{1,0:T(8,128)(2,1)}, u32[]{:S(2)}, u32[]{:S(2)}) collective-permute-start(bf16[128,4096]{1,0:T(8,128)(2,1)} %collective-permute-done.13), channel_id=1, source_target_pairs={{0,2},{2,4},{4,6},{6,32},{32,34},{34,36},{36,38},{38,0},{1,3},{3,5... | collective-permute-start | bytes 3145736 | tf_op jit(solution)/shard_map/ppermute | solution.py:170
  115.2 22.0 %collective-permute-start.16 = (bf16[128,4096]{1,0:T(8,128)(2,1)}, bf16[128,4096]{1,0:T(8,128)(2,1)}, u32[]{:S(2)}, u32[]{:S(2)}) collective-permute-start(bf16[128,4096]{1,0:T(8,128)(2,1)} %collective-permute-done.14), channel_id=1, source_target_pairs={{0,38},{2,0},{4,2},{6,4},{32,6},{34,32},{36,34},{38,36},{1,39},{3,... | collective-permute-start | bytes 3145736 | tf_op jit(solution)/shard_map/ppermute | solution.py:170
  118.6 25.0 %copy-start.2 = (bf16[4,48,4096]{2,1,0:T(8,128)(2,1)}, bf16[4,48,4096]{2,1,0:T(8,128)(2,1)S(1)}, u32[]{:S(2)}) copy-start(bf16[4,48,4096]{2,1,0:T(8,128)(2,1)S(1)} %all-to-all-done) | copy-start | bytes 4718596
  137.3 22.0 %collective-permute-start.17 = (bf16[128,4096]{1,0:T(8,128)(2,1)}, bf16[128,4096]{1,0:T(8,128)(2,1)}, u32[]{:S(2)}, u32[]{:S(2)}) collective-permute-start(bf16[128,4096]{1,0:T(8,128)(2,1)} %collective-permute-done.15), channel_id=1, source_target_pairs={{0,2},{2,4},{4,6},{6,32},{32,34},{34,36},{36,38},{38,0},{1,3},{3,5... | collective-permute-start | bytes 3145736 | tf_op jit(solution)/shard_map/ppermute | solution.py:170
  138.5 20.8 %collective-permute-start.18 = (bf16[128,4096]{1,0:T(8,128)(2,1)}, bf16[128,4096]{1,0:T(8,128)(2,1)}, u32[]{:S(2)}, u32[]{:S(2)}) collective-permute-start(bf16[128,4096]{1,0:T(8,128)(2,1)} %collective-permute-done.16), channel_id=1, source_target_pairs={{0,38},{2,0},{4,2},{6,4},{32,6},{34,32},{36,34},{38,36},{1,39},{3,... | collective-permute-start | bytes 3145736 | tf_op jit(solution)/shard_map/ppermute | solution.py:170
  145.4 16.7 %copy-start.7 = (bf16[128,4096]{1,0:T(8,128)(2,1)S(1)}, bf16[128,4096]{1,0:T(8,128)(2,1)}, u32[]{:S(2)}) copy-start(bf16[128,4096]{1,0:T(8,128)(2,1)} %get-tuple-element.68) | copy-start | bytes 3145732
  145.4 19.7 %all-to-all-start.1 = ((bf16[4,48,4096]{2,1,0:T(8,128)(2,1)}), bf16[4,48,4096]{2,1,0:T(8,128)(2,1)S(1)}, u32[]{:S(2)}, u32[]{:S(2)}) async-start(bf16[4,48,4096]{2,1,0:T(8,128)(2,1)} %bitcast.32), calls=%async_computation.1 | async-start | bytes 3145728 | tf_op jit(solution)/shard_map/all_to_all | solution.py:228
  159.3 26.1 %collective-permute-start.19 = (bf16[128,4096]{1,0:T(8,128)(2,1)}, bf16[128,4096]{1,0:T(8,128)(2,1)}, u32[]{:S(2)}, u32[]{:S(2)}) collective-permute-start(bf16[128,4096]{1,0:T(8,128)(2,1)} %collective-permute-done.17), channel_id=1, source_target_pairs={{0,2},{2,4},{4,6},{6,32},{32,34},{34,36},{36,38},{38,0},{1,3},{3,5... | collective-permute-start | bytes 3145736 | tf_op jit(solution)/shard_map/ppermute | solution.py:170
  160.4 25.0 %collective-permute-start.20 = (bf16[128,4096]{1,0:T(8,128)(2,1)}, bf16[128,4096]{1,0:T(8,128)(2,1)}, u32[]{:S(2)}, u32[]{:S(2)}) collective-permute-start(bf16[128,4096]{1,0:T(8,128)(2,1)} %collective-permute-done.18), channel_id=1, source_target_pairs={{0,38},{2,0},{4,2},{6,4},{32,6},{34,32},{36,34},{38,36},{1,39},{3,... | collective-permute-start | bytes 3145736 | tf_op jit(solution)/shard_map/ppermute | solution.py:170
  165.0 4.0 %copy-start.3 = (bf16[4,48,4096]{2,1,0:T(8,128)(2,1)}, bf16[4,48,4096]{2,1,0:T(8,128)(2,1)S(1)}, u32[]{:S(2)}) copy-start(bf16[4,48,4096]{2,1,0:T(8,128)(2,1)S(1)} %all-to-all-done.1) | copy-start | bytes 4718596
  165.0 30.3 %all-to-all-start.2 = ((bf16[4,48,4096]{2,1,0:T(8,128)(2,1)}), bf16[4,48,4096]{2,1,0:T(8,128)(2,1)S(1)}, u32[]{:S(2)}, u32[]{:S(2)}) async-start(bf16[4,48,4096]{2,1,0:T(8,128)(2,1)} %bitcast.69), calls=%async_computation.2 | async-start | bytes 3145728 | tf_op jit(solution)/shard_map/all_to_all | solution.py:228
  190.3 10.7 %collective-permute-start.21 = (bf16[48,4096]{1,0:T(8,128)(2,1)S(1)}, bf16[48,4096]{1,0:T(8,128)(2,1)S(1)}, u32[]{:S(2)}, u32[]{:S(2)}) collective-permute-start(bf16[48,4096]{1,0:T(8,128)(2,1)S(1)} %get-tuple-element.83), channel_id=1, source_target_pairs={{0,8},{8,16},{16,24},{24,0},{1,9},{9,17},{17,25},{25,1},{2,10},{10... | collective-permute-start | bytes 1179656 | tf_op jit(solution)/shard_map/ppermute | solution.py:42
  191.8 13.0 %collective-permute-start.22 = (bf16[48,4096]{1,0:T(8,128)(2,1)S(1)}, bf16[48,4096]{1,0:T(8,128)(2,1)}, u32[]{:S(2)}, u32[]{:S(2)}) collective-permute-start(bf16[48,4096]{1,0:T(8,128)(2,1)S(1)} %get-tuple-element.82), channel_id=1, source_target_pairs={{0,16},{8,24},{16,0},{24,8},{1,17},{9,25},{17,1},{25,9},{2,18},{10... | collective-permute-start | bytes 1179656 | tf_op jit(solution)/shard_map/ppermute | solution.py:42
  194.2 10.6 %collective-permute-start.23 = (bf16[48,4096]{1,0:T(8,128)(2,1)S(1)}, bf16[48,4096]{1,0:T(8,128)(2,1)}, u32[]{:S(2)}, u32[]{:S(2)}) collective-permute-start(bf16[48,4096]{1,0:T(8,128)(2,1)S(1)} %get-tuple-element.81), channel_id=1, source_target_pairs={{0,24},{8,0},{16,8},{24,16},{1,25},{9,1},{17,9},{25,17},{2,26},{10... | collective-permute-start | bytes 1179656 | tf_op jit(solution)/shard_map/ppermute | solution.py:42
  195.4 1.2 copy-start.4
  196.5 76.8 %all-to-all-start.4 = ((bf16[16,24,4096]{2,1,0:T(8,128)(2,1)}), bf16[16,24,4096]{2,1,0:T(8,128)(2,1)}, u32[]{:S(2)}, u32[]{:S(2)}) async-start(bf16[16,24,4096]{2,1,0:T(8,128)(2,1)} %bitcast.42), calls=%async_computation.4 | async-start | bytes 6291456 | tf_op jit(solution)/shard_map/all_to_all | solution.py:233
  201.0 3.8 %copy-start.12 = (bf16[48,4096]{1,0:T(8,128)(2,1)}, bf16[48,4096]{1,0:T(8,128)(2,1)S(1)}, u32[]{:S(2)}) copy-start(bf16[48,4096]{1,0:T(8,128)(2,1)S(1)} %collective-permute-done.21.refs_2_) | copy-start | bytes 1179652
  273.3 3.9 %copy-start.8 = (bf16[256,384]{1,0:T(8,128)(2,1)S(1)}, bf16[256,384]{1,0:T(8,128)(2,1)}, u32[]{:S(2)}) copy-start(bf16[256,384]{1,0:T(8,128)(2,1)} %pad_maximum_fusion) | copy-start | bytes 589828
  273.3 76.1 %all-to-all-start.3 = ((bf16[16,24,4096]{2,1,0:T(8,128)(2,1)}), bf16[16,24,4096]{2,1,0:T(8,128)(2,1)S(1)}, u32[]{:S(2)}, u32[]{:S(2)}) async-start(bf16[16,24,4096]{2,1,0:T(8,128)(2,1)} %bitcast.67), calls=%async_computation.3 | async-start | bytes 6291456 | tf_op jit(solution)/shard_map/all_to_all | solution.py:233
  349.4 1.2 copy-start
  350.6 1.2 copy-start.1

commit v4 on v3

--- a/solution.py
+++ b/solution.py
@@ -181,7 +181,7 @@
     first = choose(act_rev, act_fwd)
     hop = [((y - 1) % Y * 2 + 1, y * 2 + 1) for y in range(Y)]
     hop += [((y + 1) % Y * 2, y * 2) for y in range(Y)]
-    second = lax.ppermute(choose(act_fwd, act_rev), ("y", "z_hi"), hop)
+    second = lax.ppermute(choose(after(act_fwd, first), act_rev), ("y", "z_hi"), hop)
 
     ids = [choose(ids_fwd[0], ids_rev[0]), choose(ids_rev[0], ids_fwd[0])]
     probs = [choose(probs_fwd[0], probs_rev[0]), choose(probs_rev[0], probs_fwd[0])]
@@ -265,7 +265,7 @@
     got_a2 = all_x(after(picked(group(1, True), 1, sources[:2], 0), got_b))
     back_1 = back(after(done_1, got_a2))
     got_b2 = over_x(picked(group(1, False), 1, sources[2:], x))
-    done_2 = expert([got_a2, *got_b2], order_2, gates, ups, downs, 2 * 10**11)
+    done_2 = expert([got_a2, *got_b2], order_2, gates, ups, downs, 48 * 10**9)
     out_1 = combine(home(0), after(back_1, done_2), mixes[0])
     out_a, out_b = finish(upper, home(1), back(done_2), mixes[1], out_1)
     return out_a[None], out_b[None]

time: 356 us -> 355 us (level)
  waiting for transfers between devices: 222 us -> 211 us
    all_to_all x2, waiting for transfers between devices: 118 us -> 71 us  [back(): lax.all_to_all(done.reshape(EXPERTS, CAP, -1), ('x', 'z_lo'), split_axis=...]
    ppermute x3, waiting for transfers between devices: 3.77 us -> 42.6 us  [over_x(): lax.ppermute(blocks[i], 'x', [(j, (j + i) % X) for j in range(X)])]
    unnamed x30 -> x54, local copies, waits for them, and re-layouts: 5.74 us -> 7.48 us
  transfers between devices with their start and end apart: 29 -> 29, of which waited for: 11 -> 14; matrix products, arithmetic and copies ran while one was open for 10% -> 12% of each run, Pallas kernels for 9% -> 9%
where the time goes in v4:
time: 355 us; the launch traced here: 354 us
  waiting for transfers between devices  211 us (59%)
  starting transfers between devices  57.5 us (16%)
  Pallas kernels  35.8 us (10%)
  other arithmetic  24.1 us (7%)
  local copies, waits for them, and re-layouts  12.5 us (4%)
  matrix products  12.2 us (3%)
    ppermute x14, waiting for transfers between devices, shift_ring(): lax.ppermute(block, ('z_hi', 'z_lo'), [(i, (i + by) % n) for i in range(n)])  78.8 us
    all_to_all x2, waiting for transfers between devices, back(): lax.all_to_all(done.reshape(EXPERTS, CAP, -1), ('x', 'z_lo'), split_axis=...  71 us
    ppermute x3, waiting for transfers between devices, over_x(): lax.ppermute(blocks[i], 'x', [(j, (j + i) % X) for j in range(X)])  42.6 us
    pallas_call x2, Pallas kernels, expert(): pl.pallas_call(lambda *refs: expert_kernel(len(parts), *refs), grid=(2 *...  32.5 us
    ppermute x14, starting transfers between devices, shift_ring(): lax.ppermute(block, ('z_hi', 'z_lo'), [(i, (i + by) % n) for i in range(n)])  20.2 us
    ppermute x3, waiting for transfers between devices, body(): lax.ppermute(mine, 'z_lo', [(j, (j + i) % Z) for j in range(Z)])  18.2 us
    all_to_all x3, starting transfers between devices, all_x(): lax.all_to_all(sent.reshape(X, -1, sent.shape[1]), 'x', split_axis=0, con...  12.2 us
    all_to_all x2, starting transfers between devices, back(): lax.all_to_all(done.reshape(EXPERTS, CAP, -1), ('x', 'z_lo'), split_axis=...  10.3 us
  transfers between devices with their start and end apart: 29, of which 14 were waited for; matrix products, arithmetic and copies ran while one was open for 12% of the time, Pallas kernels for 9%

profile of v4, /device:TPU:1, one launch (start us, length us, event | category | flops | bytes accessed | tf_op | source)
XLA Modules:
  0.0 353.9 jit_solution(18282706195355827207)
XLA Ops:
  0.6 3.3 collective-permute-start.2
  4.1 2.6 bitcast_select_fusion.1
  6.7 3.9 %collective-permute-start.1 = (bf16[128,4096]{1,0:T(8,128)(2,1)}, bf16[128,4096]{1,0:T(8,128)(2,1)S(1)}, u32[]{:S(2)}, u32[]{:S(2)}) collective-permute-start(bf16[128,4096]{1,0:T(8,128)(2,1)} %bitcast_select_fusion.1), channel_id=1, source_target_pairs={{0,38},{2,0},{4,2},{6,4},{32,6},{34,32},{36,34},{38,36},{1,39},{3,... | collective-permute-start | bytes 3145736 | tf_op jit(solution)/shard_map/ppermute | solution.py:170
  11.7 2.7 collective-permute-start.6
  16.0 18.0 %collective-permute-done = bf16[128,4096]{1,0:T(8,128)(2,1)} collective-permute-done((bf16[128,4096]{1,0:T(8,128)(2,1)}, bf16[128,4096]{1,0:T(8,128)(2,1)}, u32[]{:S(2)}, u32[]{:S(2)}) %collective-permute-start) | collective-permute-done | bytes 1048608 | tf_op jit(solution)/shard_map/ppermute | solution.py:170
  36.0 2.7 collective-permute-start.4
  39.3 1.5 copy.73
  40.8 1.5 copy.74
  44.6 17.5 %collective-permute-done.3 = bf16[128,4096]{1,0:T(8,128)(2,1)S(1)} collective-permute-done((bf16[128,4096]{1,0:T(8,128)(2,1)}, bf16[128,4096]{1,0:T(8,128)(2,1)S(1)}, u32[]{:S(2)}, u32[]{:S(2)}) %collective-permute-start.3) | collective-permute-done | bytes 1048608 | tf_op jit(solution)/shard_map/ppermute | solution.py:170
  62.2 1.5 broadcast_select_fusion.1
  63.7 1.3 collective-permute-start.7
  64.9 1.4 collective-permute-start.8
  67.2 2.8 collective-permute-start.12
  70.0 18.2 %collective-permute-done.12 = s32[2,128,2]{1,2,0:T(2,128)S(1)} collective-permute-done((s32[2,128,2]{1,2,0:T(2,128)S(1)}, s32[2,128,2]{1,2,0:T(2,128)S(1)}, u32[]{:S(2)}, u32[]{:S(2)}) %collective-permute-start.12) | collective-permute-done | bytes 2080 | tf_op jit(solution)/shard_map/ppermute | solution.py:192
  89.0 2.5 collective-permute-start.13
  91.8 1.8 select_select_fusion.7
  93.7 1.8 convolution_convert_fusion.3
  95.5 4.0 %all-to-all-start = ((bf16[4,48,4096]{2,1,0:T(8,128)(2,1)}), bf16[4,48,4096]{2,1,0:T(8,128)(2,1)S(1)}, u32[]{:S(2)}, u32[]{:S(2)}) async-start(bf16[4,48,4096]{2,1,0:T(8,128)(2,1)} %bitcast.75), calls=%async_computation | async-start | bytes 3145728 | tf_op jit(solution)/shard_map/all_to_all | solution.py:228
  99.5 12.8 %collective-permute-done.13 = bf16[128,4096]{1,0:T(8,128)(2,1)} collective-permute-done((bf16[128,4096]{1,0:T(8,128)(2,1)S(1)}, bf16[128,4096]{1,0:T(8,128)(2,1)}, u32[]{:S(2)}, u32[]{:S(2)}) %collective-permute-start.13) | collective-permute-done | bytes 1048608 | tf_op jit(solution)/shard_map/ppermute | solution.py:170
  112.3 1.8 collective-permute-done.14
  115.1 1.8 collective-permute-start.16
  118.5 18.6 %collective-permute-done.15 = bf16[128,4096]{1,0:T(8,128)(2,1)} collective-permute-done((bf16[128,4096]{1,0:T(8,128)(2,1)}, bf16[128,4096]{1,0:T(8,128)(2,1)}, u32[]{:S(2)}, u32[]{:S(2)}) %collective-permute-start.15) | collective-permute-done | bytes 1048608 | tf_op jit(solution)/shard_map/ppermute | solution.py:170
  137.1 1.6 collective-permute-start.17
  139.9 3.7 %select_select_fusion.3 = (bf16[128,4096]{1,0:T(8,128)(2,1)}, bf16[128,4096]{1,0:T(8,128)(2,1)S(1)}, bf16[128,4096]{1,0:T(8,128)(2,1)S(1)}, bf16[128,4096]{1,0:T(8,128)(2,1)}) fusion(bf16[128,4096]{1,0:T(8,128)(2,1)} %collective-permute-done.8, bf16[128,4096]{1,0:T(8,128)(2,1)} %collective-permute-done.14, bf16[128,4096]{1,0:T(8,128)(2,1)S(1)} %collective-permute-done.7, ...), kind=kLoop, calls=%fused_computation.28 | loop fusion | flops 6291456 | bytes 10485762 | tf_op jit(solution)/shard_map/jit(_where)/select_n | solution.py:218
  143.6 1.8 convolution_convert_fusion.2
  145.3 4.1 %all-to-all-start.1 = ((bf16[4,48,4096]{2,1,0:T(8,128)(2,1)}), bf16[4,48,4096]{2,1,0:T(8,128)(2,1)S(1)}, u32[]{:S(2)}, u32[]{:S(2)}) async-start(bf16[4,48,4096]{2,1,0:T(8,128)(2,1)} %bitcast.32), calls=%async_computation.1 | async-start | bytes 3145728 | tf_op jit(solution)/shard_map/all_to_all | solution.py:228
  149.5 9.8 %collective-permute-done.17 = bf16[128,4096]{1,0:T(8,128)(2,1)} collective-permute-done((bf16[128,4096]{1,0:T(8,128)(2,1)}, bf16[128,4096]{1,0:T(8,128)(2,1)}, u32[]{:S(2)}, u32[]{:S(2)}) %collective-permute-start.17) | collective-permute-done | bytes 1048608 | tf_op jit(solution)/shard_map/ppermute | solution.py:170
  160.3 1.8 collective-permute-start.20
  162.7 3.0 convolution_convert_fusion.1
  165.7 4.0 %all-to-all-start.2 = ((bf16[4,48,4096]{2,1,0:T(8,128)(2,1)}), bf16[4,48,4096]{2,1,0:T(8,128)(2,1)S(1)}, u32[]{:S(2)}, u32[]{:S(2)}) async-start(bf16[4,48,4096]{2,1,0:T(8,128)(2,1)} %bitcast.76), calls=%async_computation.2 | async-start | bytes 3145728 | tf_op jit(solution)/shard_map/all_to_all | solution.py:228
  170.3 16.3 %expert.2 = bf16[384,4096]{1,0:T(8,128)(2,1)} custom-call(bf16[192,4096]{1,0:T(8,128)(2,1)} %bitcast.61, bf16[192,4096]{1,0:T(8,128)(2,1)} %bitcast.62, bf16[384,384]{1,0:T(8,128)(2,1)} %fusion.16.refs_2_, bf16[4096,384]{1,0:T(8,128)(2,1)} %bitcast.65, bf16[4096,384]{1,0:T(8,128)(2,1)} %collective-permute-done.2.refs_4_.refs_7_, bf16[4096,384]{1,0:T(8,128)(2,1)} %bitcast.68, ...), custom_call_target="tpu_custom_call" | custom-call | flops 100000000 | bytes 1000000 | tf_op jit(solution)/shard_map/expert/pallas_call | solution.py:100
  186.6 4.1 %select_select_fusion.1 = (bf16[128,4096]{1,0:T(8,128)(2,1)}, bf16[128,4096]{1,0:T(8,128)(2,1)}, bf16[128,4096]{1,0:T(8,128)(2,1)}) fusion(bf16[128,4096]{1,0:T(8,128)(2,1)} %collective-permute-done.17, bf16[128,4096]{1,0:T(8,128)(2,1)} %collective-permute-done.15, bf16[128,4096]{1,0:T(8,128)(2,1)} %collective-permute-done.18, ...), kind=kLoop, calls=%fused_computation.26 | loop fusion | flops 3670016 | bytes 9437186 | tf_op jit(solution)/shard_map/jit(_where)/select_n | solution.py:218
  191.8 6.5 %all-to-all-start.4 = ((bf16[16,24,4096]{2,1,0:T(8,128)(2,1)}), bf16[16,24,4096]{2,1,0:T(8,128)(2,1)S(1)}, u32[]{:S(2)}, u32[]{:S(2)}) async-start(bf16[16,24,4096]{2,1,0:T(8,128)(2,1)} %bitcast.42), calls=%async_computation.4 | async-start | bytes 6291456 | tf_op jit(solution)/shard_map/all_to_all | solution.py:233
  198.4 2.2 convolution_convert_fusion
  201.4 1.4 collective-permute-start.21
  202.8 2.4 collective-permute-start.22
  206.4 32.4 %collective-permute-done.21.refs_2_ = bf16[48,4096]{1,0:T(8,128)(2,1)S(1)} collective-permute-done((bf16[48,4096]{1,0:T(8,128)(2,1)S(1)}, bf16[48,4096]{1,0:T(8,128)(2,1)S(1)}, u32[]{:S(2)}, u32[]{:S(2)}) %collective-permute-start.21) | collective-permute-done | bytes 393248 | tf_op jit(solution)/shard_map/ppermute | solution.py:42
  238.7 8.8 %collective-permute-done.22.refs_3_ = bf16[48,4096]{1,0:T(8,128)(2,1)S(1)} collective-permute-done((bf16[48,4096]{1,0:T(8,128)(2,1)S(1)}, bf16[48,4096]{1,0:T(8,128)(2,1)S(1)}, u32[]{:S(2)}, u32[]{:S(2)}) %collective-permute-start.22) | collective-permute-done | bytes 393248 | tf_op jit(solution)/shard_map/ppermute | solution.py:42
  247.5 1.4 collective-permute-done.23.refs_4_
  249.7 16.2 %expert.3 = bf16[384,4096]{1,0:T(8,128)(2,1)} custom-call(bf16[192,4096]{1,0:T(8,128)(2,1)} %bitcast.74, bf16[48,4096]{1,0:T(8,128)(2,1)} %get-tuple-element.84.refs_1_, bf16[48,4096]{1,0:T(8,128)(2,1)} %copy-done.20, bf16[48,4096]{1,0:T(8,128)(2,1)} %copy-done.21, bf16[48,4096]{1,0:T(8,128)(2,1)} %copy-done.22, bf16[384,384]{1,0:T(8,128)(2,1)} %fusion.17.refs_5_, ...), custom_call_target="tpu_custom_call" | custom-call | flops 48000000000 | bytes 1000000 | tf_op jit(solution)/shard_map/expert/pallas_call | solution.py:100
  265.9 4.6 %all-to-all-done.4 = bf16[16,24,4096]{2,1,0:T(8,128)(2,1)S(1)} async-done(((bf16[16,24,4096]{2,1,0:T(8,128)(2,1)}), bf16[16,24,4096]{2,1,0:T(8,128)(2,1)S(1)}, u32[]{:S(2)}, u32[]{:S(2)}) %all-to-all-start.4) | async-done | bytes 3145760 | tf_op jit(solution)/shard_map/all_to_all | solution.py:233
  270.6 1.6 copy-done.2
  272.2 3.7 %all-to-all-start.3 = ((bf16[16,24,4096]{2,1,0:T(8,128)(2,1)}), bf16[16,24,4096]{2,1,0:T(8,128)(2,1)S(1)}, u32[]{:S(2)}, u32[]{:S(2)}) async-start(bf16[16,24,4096]{2,1,0:T(8,128)(2,1)} %bitcast.73), calls=%async_computation.3 | async-start | bytes 6291456 | tf_op jit(solution)/shard_map/all_to_all | solution.py:233
  275.9 3.1 fusion.100
  279.1 2.7 fusion.1.other
  281.8 66.4 %all-to-all-done.3 = bf16[16,24,4096]{2,1,0:T(8,128)(2,1)S(1)} async-done(((bf16[16,24,4096]{2,1,0:T(8,128)(2,1)}), bf16[16,24,4096]{2,1,0:T(8,128)(2,1)S(1)}, u32[]{:S(2)}, u32[]{:S(2)}) %all-to-all-start.3) | async-done | bytes 3145760 | tf_op jit(solution)/shard_map/all_to_all | solution.py:233
  348.2 1.2 copy-done
  350.6 3.2 finish.1
  (122 shorter events, 20.6 us)
Async XLA Ops:
  0.6 10.0 %copy-start.6 = (bf16[1,128,4096]{2,1,0:T(8,128)(2,1)S(1)}, bf16[1,128,4096]{2,1,0:T(8,128)(2,1)}, u32[]{:S(2)}) copy-start(bf16[1,128,4096]{2,1,0:T(8,128)(2,1)} %param.10) | copy-start | bytes 3145732
  0.6 10.0 %copy-start.5 = (bf16[1,128,4096]{2,1,0:T(8,128)(2,1)S(1)}, bf16[1,128,4096]{2,1,0:T(8,128)(2,1)}, u32[]{:S(2)}) copy-start(bf16[1,128,4096]{2,1,0:T(8,128)(2,1)} %param.9) | copy-start | bytes 3145732
  0.6 34.3 %collective-permute-start.2 = (bf16[4096,384]{1,0:T(8,128)(2,1)}, bf16[4096,384]{1,0:T(8,128)(2,1)}, u32[]{:S(2)}, u32[]{:S(2)}) collective-permute-start(bf16[4096,384]{1,0:T(8,128)(2,1)} %bitcast.64), channel_id=1, source_target_pairs={{0,1},{1,0},{2,3},{3,2},{4,5},{5,4},{6,7},{7,6},{8,9},{9,8},{10,11... | collective-permute-start | bytes 9437192 | tf_op jit(solution)/shard_map/ppermute | solution.py:196
  4.0 40.5 %collective-permute-start.5 = (bf16[4096,384]{1,0:T(8,128)(2,1)}, bf16[4096,384]{1,0:T(8,128)(2,1)}, u32[]{:S(2)}, u32[]{:S(2)}) collective-permute-start(bf16[4096,384]{1,0:T(8,128)(2,1)} %bitcast.67), channel_id=1, source_target_pairs={{0,1},{1,0},{2,3},{3,2},{4,5},{5,4},{6,7},{7,6},{8,9},{9,8},{10,11... | collective-permute-start | bytes 9437192 | tf_op jit(solution)/shard_map/ppermute | solution.py:196
  6.7 7.8 %copy-start.10 = (s32[1,128,2]{1,2,0:T(2,128)S(1)}, s32[1,128,2]{1,2,0:T(2,128)}, u32[]{:S(2)}) copy-start(s32[1,128,2]{1,2,0:T(2,128)} %param.11) | copy-start | bytes 3076
  6.7 7.9 %copy-start.11 = (s32[1,128,2]{1,2,0:T(2,128)S(1)}, s32[1,128,2]{1,2,0:T(2,128)}, u32[]{:S(2)}) copy-start(s32[1,128,2]{1,2,0:T(2,128)} %param.12) | copy-start | bytes 3076
  6.7 27.3 %collective-permute-start = (bf16[128,4096]{1,0:T(8,128)(2,1)}, bf16[128,4096]{1,0:T(8,128)(2,1)}, u32[]{:S(2)}, u32[]{:S(2)}) collective-permute-start(bf16[128,4096]{1,0:T(8,128)(2,1)} %bitcast_select_fusion.1), channel_id=1, source_target_pairs={{0,2},{2,4},{4,6},{6,32},{32,34},{34,36},{36,38},{38,0},{1,3},{3,5... | collective-permute-start | bytes 3145736 | tf_op jit(solution)/shard_map/ppermute | solution.py:170
  6.7 28.3 %collective-permute-start.1 = (bf16[128,4096]{1,0:T(8,128)(2,1)}, bf16[128,4096]{1,0:T(8,128)(2,1)S(1)}, u32[]{:S(2)}, u32[]{:S(2)}) collective-permute-start(bf16[128,4096]{1,0:T(8,128)(2,1)} %bitcast_select_fusion.1), channel_id=1, source_target_pairs={{0,38},{2,0},{4,2},{6,4},{32,6},{34,32},{36,34},{38,36},{1,39},{3,... | collective-permute-start | bytes 3145736 | tf_op jit(solution)/shard_map/ppermute | solution.py:170
  10.6 31.7 %copy-start.12 = (f32[1,128,2]{1,2,0:T(2,128)S(1)}, f32[1,128,2]{1,2,0:T(2,128)}, u32[]{:S(2)}) copy-start(f32[1,128,2]{1,2,0:T(2,128)} %param.13) | copy-start | bytes 3076
  10.6 31.9 %copy-start.13 = (f32[1,128,2]{1,2,0:T(2,128)S(1)}, f32[1,128,2]{1,2,0:T(2,128)}, u32[]{:S(2)}) copy-start(f32[1,128,2]{1,2,0:T(2,128)} %param.14) | copy-start | bytes 3076
  11.7 50.4 %collective-permute-start.6 = (bf16[128,4096]{1,0:T(8,128)(2,1)}, bf16[128,4096]{1,0:T(8,128)(2,1)S(1)}, u32[]{:S(2)}, u32[]{:S(2)}) collective-permute-start(bf16[128,4096]{1,0:T(8,128)(2,1)} %bitcast_select_fusion), channel_id=1, source_target_pairs={{224,32},{32,96},{96,160},{160,224},{64,0},{128,64},{192,128},{0,1... | collective-permute-start | bytes 3145736 | tf_op jit(solution)/shard_map/ppermute | solution.py:184
  34.0 54.9 %collective-permute-start.9 = (bf16[384,4096]{1,0:T(8,128)(2,1)}, bf16[384,4096]{1,0:T(8,128)(2,1)}, u32[]{:S(2)}, u32[]{:S(2)}) collective-permute-start(bf16[384,4096]{1,0:T(8,128)(2,1)} %bitcast.70), channel_id=1, source_target_pairs={{0,1},{1,0},{2,3},{3,2},{4,5},{5,4},{6,7},{7,6},{8,9},{9,8},{10,11... | collective-permute-start | bytes 9437192 | tf_op jit(solution)/shard_map/ppermute | solution.py:196
  35.9 26.2 %collective-permute-start.3 = (bf16[128,4096]{1,0:T(8,128)(2,1)}, bf16[128,4096]{1,0:T(8,128)(2,1)S(1)}, u32[]{:S(2)}, u32[]{:S(2)}) collective-permute-start(bf16[128,4096]{1,0:T(8,128)(2,1)} %collective-permute-done), channel_id=1, source_target_pairs={{0,2},{2,4},{4,6},{6,32},{32,34},{34,36},{36,38},{38,0},{1,3},{3,5... | collective-permute-start | bytes 3145736 | tf_op jit(solution)/shard_map/ppermute | solution.py:170
  36.0 26.2 %collective-permute-start.4 = (bf16[128,4096]{1,0:T(8,128)(2,1)}, bf16[128,4096]{1,0:T(8,128)(2,1)S(1)}, u32[]{:S(2)}, u32[]{:S(2)}) collective-permute-start(bf16[128,4096]{1,0:T(8,128)(2,1)} %copy-done.8), channel_id=1, source_target_pairs={{0,38},{2,0},{4,2},{6,4},{32,6},{34,32},{36,34},{38,36},{1,39},{3,... | collective-permute-start | bytes 3145736 | tf_op jit(solution)/shard_map/ppermute | solution.py:170
  44.5 22.7 %collective-permute-start.10 = (s32[2,128,2]{1,2,0:T(2,128)S(1)}, s32[2,128,2]{1,2,0:T(2,128)S(1)}, u32[]{:S(2)}, u32[]{:S(2)}) collective-permute-start(s32[2,128,2]{1,2,0:T(2,128)S(1)} %pad_add_fusion.1), channel_id=1, source_target_pairs={{0,2},{2,4},{4,6},{6,0},{1,3},{3,5},{5,7},{7,1},{8,10},{10,12},{12... | collective-permute-start | bytes 6152 | tf_op jit(solution)/shard_map/ppermute | solution.py:192
  62.2 7.8 %collective-permute-start.11 = (s32[2,128,2]{1,2,0:T(2,128)S(1)}, s32[2,128,2]{1,2,0:T(2,128)}, u32[]{:S(2)}, u32[]{:S(2)}) collective-permute-start(s32[2,128,2]{1,2,0:T(2,128)S(1)} %pad_add_fusion.1), channel_id=1, source_target_pairs={{0,4},{2,6},{4,0},{6,2},{1,5},{3,7},{5,1},{7,3},{8,12},{10,14},{12... | collective-permute-start | bytes 6152 | tf_op jit(solution)/shard_map/ppermute | solution.py:192
  63.7 25.3 %collective-permute-start.7 = (bf16[128,4096]{1,0:T(8,128)(2,1)}, bf16[128,4096]{1,0:T(8,128)(2,1)S(1)}, u32[]{:S(2)}, u32[]{:S(2)}) collective-permute-start(bf16[128,4096]{1,0:T(8,128)(2,1)} %get-tuple-element.86), channel_id=1, source_target_pairs={{0,2},{2,4},{4,6},{6,32},{32,34},{34,36},{36,38},{38,0},{1,3},{3,5... | collective-permute-start | bytes 3145736 | tf_op jit(solution)/shard_map/ppermute | solution.py:170
  64.9 24.1 %collective-permute-start.8 = (bf16[128,4096]{1,0:T(8,128)(2,1)}, bf16[128,4096]{1,0:T(8,128)(2,1)}, u32[]{:S(2)}, u32[]{:S(2)}) collective-permute-start(bf16[128,4096]{1,0:T(8,128)(2,1)} %get-tuple-element.85), channel_id=1, source_target_pairs={{0,38},{2,0},{4,2},{6,4},{32,6},{34,32},{36,34},{38,36},{1,39},{3,... | collective-permute-start | bytes 3145736 | tf_op jit(solution)/shard_map/ppermute | solution.py:170
  67.2 21.0 %collective-permute-start.12 = (s32[2,128,2]{1,2,0:T(2,128)S(1)}, s32[2,128,2]{1,2,0:T(2,128)S(1)}, u32[]{:S(2)}, u32[]{:S(2)}) collective-permute-start(s32[2,128,2]{1,2,0:T(2,128)S(1)} %pad_add_fusion.1), channel_id=1, source_target_pairs={{0,6},{2,0},{4,2},{6,4},{1,7},{3,1},{5,3},{7,5},{8,14},{10,8},{12,... | collective-permute-start | bytes 6152 | tf_op jit(solution)/shard_map/ppermute | solution.py:192
  89.0 23.3 %collective-permute-start.13 = (bf16[128,4096]{1,0:T(8,128)(2,1)S(1)}, bf16[128,4096]{1,0:T(8,128)(2,1)}, u32[]{:S(2)}, u32[]{:S(2)}) collective-permute-start(bf16[128,4096]{1,0:T(8,128)(2,1)S(1)} %collective-permute-done.7), channel_id=1, source_target_pairs={{0,2},{2,4},{4,6},{6,32},{32,34},{34,36},{36,38},{38,0},{1,3},{3,5... | collective-permute-start | bytes 3145736 | tf_op jit(solution)/shard_map/ppermute | solution.py:170
  91.5 22.7 %collective-permute-start.14 = (bf16[128,4096]{1,0:T(8,128)(2,1)}, bf16[128,4096]{1,0:T(8,128)(2,1)}, u32[]{:S(2)}, u32[]{:S(2)}) collective-permute-start(bf16[128,4096]{1,0:T(8,128)(2,1)} %collective-permute-done.8), channel_id=1, source_target_pairs={{0,38},{2,0},{4,2},{6,4},{32,6},{34,32},{36,34},{38,36},{1,39},{3,... | collective-permute-start | bytes 3145736 | tf_op jit(solution)/shard_map/ppermute | solution.py:170
  91.8 1.9 copy-start.14
  91.8 1.9 copy-start.15
  91.8 1.9 copy-start.23
  95.5 23.0 %all-to-all-start = ((bf16[4,48,4096]{2,1,0:T(8,128)(2,1)}), bf16[4,48,4096]{2,1,0:T(8,128)(2,1)S(1)}, u32[]{:S(2)}, u32[]{:S(2)}) async-start(bf16[4,48,4096]{2,1,0:T(8,128)(2,1)} %bitcast.75), calls=%async_computation | async-start | bytes 3145728 | tf_op jit(solution)/shard_map/all_to_all | solution.py:228
  114.1 23.0 %collective-permute-start.15 = (bf16[128,4096]{1,0:T(8,128)(2,1)}, bf16[128,4096]{1,0:T(8,128)(2,1)}, u32[]{:S(2)}, u32[]{:S(2)}) collective-permute-start(bf16[128,4096]{1,0:T(8,128)(2,1)} %collective-permute-done.13), channel_id=1, source_target_pairs={{0,2},{2,4},{4,6},{6,32},{32,34},{34,36},{36,38},{38,0},{1,3},{3,5... | collective-permute-start | bytes 3145736 | tf_op jit(solution)/shard_map/ppermute | solution.py:170
  115.1 22.1 %collective-permute-start.16 = (bf16[128,4096]{1,0:T(8,128)(2,1)}, bf16[128,4096]{1,0:T(8,128)(2,1)}, u32[]{:S(2)}, u32[]{:S(2)}) collective-permute-start(bf16[128,4096]{1,0:T(8,128)(2,1)} %collective-permute-done.14), channel_id=1, source_target_pairs={{0,38},{2,0},{4,2},{6,4},{32,6},{34,32},{36,34},{38,36},{1,39},{3,... | collective-permute-start | bytes 3145736 | tf_op jit(solution)/shard_map/ppermute | solution.py:170
  118.5 25.1 %copy-start.3 = (bf16[4,48,4096]{2,1,0:T(8,128)(2,1)}, bf16[4,48,4096]{2,1,0:T(8,128)(2,1)S(1)}, u32[]{:S(2)}) copy-start(bf16[4,48,4096]{2,1,0:T(8,128)(2,1)S(1)} %all-to-all-done) | copy-start | bytes 4718596
  137.1 6.4 %copy-start.16 = (s32[192]{0:T(256)S(1)}, s32[192]{0:T(256)}, u32[]{:S(2)}) copy-start(s32[192]{0:T(256)} %get-tuple-element.120) | copy-start | bytes 2308
  137.1 6.4 %copy-start.24 = (s32[256]{0:T(256)S(1)}, s32[256]{0:T(256)}, u32[]{:S(2)}) copy-start(s32[256]{0:T(256)} %and_select_fusion.3) | copy-start | bytes 3076
  137.1 22.1 %collective-permute-start.17 = (bf16[128,4096]{1,0:T(8,128)(2,1)}, bf16[128,4096]{1,0:T(8,128)(2,1)}, u32[]{:S(2)}, u32[]{:S(2)}) collective-permute-start(bf16[128,4096]{1,0:T(8,128)(2,1)} %collective-permute-done.15), channel_id=1, source_target_pairs={{0,2},{2,4},{4,6},{6,32},{32,34},{34,36},{36,38},{38,0},{1,3},{3,5... | collective-permute-start | bytes 3145736 | tf_op jit(solution)/shard_map/ppermute | solution.py:170
  138.8 20.6 %collective-permute-start.18 = (bf16[128,4096]{1,0:T(8,128)(2,1)}, bf16[128,4096]{1,0:T(8,128)(2,1)}, u32[]{:S(2)}, u32[]{:S(2)}) collective-permute-start(bf16[128,4096]{1,0:T(8,128)(2,1)} %collective-permute-done.16), channel_id=1, source_target_pairs={{0,38},{2,0},{4,2},{6,4},{32,6},{34,32},{36,34},{38,36},{1,39},{3,... | collective-permute-start | bytes 3145736 | tf_op jit(solution)/shard_map/ppermute | solution.py:170
  145.3 17.3 %copy-start.9 = (bf16[128,4096]{1,0:T(8,128)(2,1)S(1)}, bf16[128,4096]{1,0:T(8,128)(2,1)}, u32[]{:S(2)}) copy-start(bf16[128,4096]{1,0:T(8,128)(2,1)} %get-tuple-element.70) | copy-start | bytes 3145732
  145.3 20.3 %all-to-all-start.1 = ((bf16[4,48,4096]{2,1,0:T(8,128)(2,1)}), bf16[4,48,4096]{2,1,0:T(8,128)(2,1)S(1)}, u32[]{:S(2)}, u32[]{:S(2)}) async-start(bf16[4,48,4096]{2,1,0:T(8,128)(2,1)} %bitcast.32), calls=%async_computation.1 | async-start | bytes 3145728 | tf_op jit(solution)/shard_map/all_to_all | solution.py:228
  159.4 27.2 %collective-permute-start.19 = (bf16[128,4096]{1,0:T(8,128)(2,1)}, bf16[128,4096]{1,0:T(8,128)(2,1)}, u32[]{:S(2)}, u32[]{:S(2)}) collective-permute-start(bf16[128,4096]{1,0:T(8,128)(2,1)} %collective-permute-done.17), channel_id=1, source_target_pairs={{0,2},{2,4},{4,6},{6,32},{32,34},{34,36},{36,38},{38,0},{1,3},{3,5... | collective-permute-start | bytes 3145736 | tf_op jit(solution)/shard_map/ppermute | solution.py:170
  160.3 26.3 %collective-permute-start.20 = (bf16[128,4096]{1,0:T(8,128)(2,1)}, bf16[128,4096]{1,0:T(8,128)(2,1)}, u32[]{:S(2)}, u32[]{:S(2)}) collective-permute-start(bf16[128,4096]{1,0:T(8,128)(2,1)} %collective-permute-done.18), channel_id=1, source_target_pairs={{0,38},{2,0},{4,2},{6,4},{32,6},{34,32},{36,34},{38,36},{1,39},{3,... | collective-permute-start | bytes 3145736 | tf_op jit(solution)/shard_map/ppermute | solution.py:170
  165.7 4.6 %copy-start.4 = (bf16[4,48,4096]{2,1,0:T(8,128)(2,1)}, bf16[4,48,4096]{2,1,0:T(8,128)(2,1)S(1)}, u32[]{:S(2)}) copy-start(bf16[4,48,4096]{2,1,0:T(8,128)(2,1)S(1)} %all-to-all-done.1) | copy-start | bytes 4718596
  165.7 25.0 %all-to-all-start.2 = ((bf16[4,48,4096]{2,1,0:T(8,128)(2,1)}), bf16[4,48,4096]{2,1,0:T(8,128)(2,1)S(1)}, u32[]{:S(2)}, u32[]{:S(2)}) async-start(bf16[4,48,4096]{2,1,0:T(8,128)(2,1)} %bitcast.76), calls=%async_computation.2 | async-start | bytes 3145728 | tf_op jit(solution)/shard_map/all_to_all | solution.py:228
  190.6 7.7 %copy-start.17 = (s32[192]{0:T(256)S(1)}, s32[192]{0:T(256)}, u32[]{:S(2)}) copy-start(s32[192]{0:T(256)} %fusion.84) | copy-start | bytes 2308
  190.6 7.7 %copy-start.18 = (s32[256,1]{0,1:T(1,128)S(1)}, s32[256,1]{0,1:T(1,128)}, u32[]{:S(2)}) copy-start(s32[256,1]{0,1:T(1,128)} %get-tuple-element.105) | copy-start | bytes 3076
  190.6 7.7 %copy-start.19 = (s32[256,1]{0,1:T(1,128)S(1)}, s32[256,1]{0,1:T(1,128)}, u32[]{:S(2)}) copy-start(s32[256,1]{0,1:T(1,128)} %get-tuple-element.106) | copy-start | bytes 3076
  191.8 78.7 %all-to-all-start.4 = ((bf16[16,24,4096]{2,1,0:T(8,128)(2,1)}), bf16[16,24,4096]{2,1,0:T(8,128)(2,1)S(1)}, u32[]{:S(2)}, u32[]{:S(2)}) async-start(bf16[16,24,4096]{2,1,0:T(8,128)(2,1)} %bitcast.42), calls=%async_computation.4 | async-start | bytes 6291456 | tf_op jit(solution)/shard_map/all_to_all | solution.py:233
  201.4 37.3 %collective-permute-start.21 = (bf16[48,4096]{1,0:T(8,128)(2,1)S(1)}, bf16[48,4096]{1,0:T(8,128)(2,1)S(1)}, u32[]{:S(2)}, u32[]{:S(2)}) collective-permute-start(bf16[48,4096]{1,0:T(8,128)(2,1)S(1)} %get-tuple-element.83), channel_id=1, source_target_pairs={{0,8},{8,16},{16,24},{24,0},{1,9},{9,17},{17,25},{25,1},{2,10},{10... | collective-permute-start | bytes 1179656 | tf_op jit(solution)/shard_map/ppermute | solution.py:42
  202.8 44.7 %collective-permute-start.22 = (bf16[48,4096]{1,0:T(8,128)(2,1)S(1)}, bf16[48,4096]{1,0:T(8,128)(2,1)S(1)}, u32[]{:S(2)}, u32[]{:S(2)}) collective-permute-start(bf16[48,4096]{1,0:T(8,128)(2,1)S(1)} %get-tuple-element.82), channel_id=1, source_target_pairs={{0,16},{8,24},{16,0},{24,8},{1,17},{9,25},{17,1},{25,9},{2,18},{10... | collective-permute-start | bytes 1179656 | tf_op jit(solution)/shard_map/ppermute | solution.py:42
  205.2 43.7 %collective-permute-start.23 = (bf16[48,4096]{1,0:T(8,128)(2,1)S(1)}, bf16[48,4096]{1,0:T(8,128)(2,1)S(1)}, u32[]{:S(2)}, u32[]{:S(2)}) collective-permute-start(bf16[48,4096]{1,0:T(8,128)(2,1)S(1)} %get-tuple-element.81), channel_id=1, source_target_pairs={{0,24},{8,0},{16,8},{24,16},{1,25},{9,1},{17,9},{25,17},{2,26},{10... | collective-permute-start | bytes 1179656 | tf_op jit(solution)/shard_map/ppermute | solution.py:42
  238.7 10.2 %copy-start.20 = (bf16[48,4096]{1,0:T(8,128)(2,1)}, bf16[48,4096]{1,0:T(8,128)(2,1)S(1)}, u32[]{:S(2)}) copy-start(bf16[48,4096]{1,0:T(8,128)(2,1)S(1)} %collective-permute-done.21.refs_2_) | copy-start | bytes 1179652
  270.6 1.6 copy-start.2
  272.2 76.0 %all-to-all-start.3 = ((bf16[16,24,4096]{2,1,0:T(8,128)(2,1)}), bf16[16,24,4096]{2,1,0:T(8,128)(2,1)S(1)}, u32[]{:S(2)}, u32[]{:S(2)}) async-start(bf16[16,24,4096]{2,1,0:T(8,128)(2,1)} %bitcast.73), calls=%async_computation.3 | async-start | bytes 6291456 | tf_op jit(solution)/shard_map/all_to_all | solution.py:233
  (6 other events, 6.8 us)
